TPU v7x, 128 devices: a whole 4x4x4 slice. The times are simulated.
128 devices in a mesh: gx: 64 (over y, x, z_hi, core), ta: 2 (over z_lo).
Axes of the slice: x: 4, y: 4, z: 4 (z_hi: 2, z_lo: 2; z = z_hi * 2 + z_lo), core: 2. Of those that a mesh axis runs over, the one named last changes fastest.
Arguments:
- voltages: int32 [512, 524288], P('gx', 'ta'), may hold values from -128 to 127
Outputs:
- visibilities: float32 [1024, 2, 512, 512], P(('gx', 'ta'))
All inputs are finite; a program needn't handle non-finite values.
Results may differ from a plain program's by a relative error of at most 0.0052.
Values may be sent and summed in bfloat16 or wider, within the bound.
No kernel may reach another device: no remote copies, remote signals or barrier semaphores. Data moves between devices by JAX's collectives and lax.ppermute only.
A program may use at most 192 MiB of HBM per device.

v0:
```python
import math

import jax
import jax.numpy as jnp
from jax import lax
from jax.sharding import PartitionSpec as P

INPUTS = 512
CHAN = 1024
TAPS = 4


def shifted(array, axis, by):
    count = lax.axis_size(axis)
    pairs = [(i, i + by) for i in range(count) if 0 <= i + by < count]
    return lax.ppermute(array, axis, pairs)


def window_taps(frame_len):
    total_len = TAPS * frame_len
    positions = jnp.arange(total_len, dtype=jnp.float32)
    centred = (positions + 0.5 - total_len / 2.0) / frame_len
    hamming = 0.54 - 0.46 * jnp.cos(2.0 * jnp.pi * positions / (total_len - 1))
    return (jnp.sinc(centred) * hamming).reshape(TAPS, frame_len)


def dft_rows(chan_list, frame_len):
    samples_index = jnp.arange(frame_len, dtype=jnp.int32)
    phase = chan_list[:, None] * samples_index[None, :] % frame_len
    angle = phase.astype(jnp.float32) * (2.0 * jnp.pi / frame_len)
    rows = jnp.stack([jnp.cos(angle), -jnp.sin(angle)], axis=1)
    return rows.reshape(2 * chan_list.shape[0], frame_len).astype(jnp.bfloat16)


def on_device(voltages):
    gx_count = lax.axis_size("gx")
    ta_count = lax.axis_size("ta")
    inputs_here, total_len = voltages.shape
    frame_len = 2 * CHAN
    spec_here = total_len // frame_len
    per_dev = CHAN // (gx_count * ta_count)
    values = voltages.astype(jnp.bfloat16)
    tail = values[:, total_len - (TAPS - 1) * frame_len :]
    earlier = shifted(tail, "ta", 1)
    joined = jnp.concatenate([earlier, values], axis=1)
    frames = joined.reshape(inputs_here, spec_here + TAPS - 1, frame_len)
    weights = window_taps(frame_len)
    filtered = weights[0] * frames[:, 0:spec_here, :].astype(jnp.float32)
    for tap in range(1, TAPS):
        filtered = filtered + weights[tap] * frames[:, tap : tap + spec_here, :].astype(jnp.float32)
    filtered = filtered.astype(jnp.bfloat16)
    scale = 1.0 / (64.0 * math.sqrt(frame_len))
    chan_index = jnp.arange(CHAN, dtype=jnp.int32)
    dft_table = dft_rows(chan_index, frame_len)
    spectra = jnp.einsum("cf,isf->cis", dft_table, filtered, preferred_element_type=jnp.float32)
    spectra = (spectra * scale).astype(jnp.bfloat16)
    outgoing = spectra.reshape(gx_count * ta_count, per_dev, 2, inputs_here, spec_here)
    arrived = lax.all_to_all(outgoing, ("gx", "ta"), split_axis=0, concat_axis=0, tiled=True)
    arrived = arrived.reshape(gx_count, ta_count, per_dev, 2, inputs_here, spec_here)
    ordered = jnp.transpose(arrived, (2, 3, 0, 4, 1, 5))
    stacked = ordered.reshape(per_dev, 2 * INPUTS, ta_count * spec_here)
    gram = lax.dot_general(
        stacked, stacked, (((2,), (2,)), ((0,), (0,))), preferred_element_type=jnp.float32
    )
    norm_factor = 1.0 / math.sqrt(ta_count * spec_here)
    real_part = gram[:, :INPUTS, :INPUTS] + gram[:, INPUTS:, INPUTS:]
    imag_part = gram[:, INPUTS:, :INPUTS] - gram[:, :INPUTS, INPUTS:]
    return jnp.stack([real_part, imag_part], axis=1) * norm_factor


def solution(mesh):
    placed = (P("gx", "ta"),)
    return jax.shard_map(
        on_device,
        mesh=mesh,
        in_specs=placed,
        out_specs=P(("gx", "ta"), None, None, None),
        check_vma=False,
    )
```

profile of v0, /device:TPU:1, one launch (start us, length us, event | category | flops | bytes accessed | tf_op | source)
XLA Modules:
  0.0 294.0 jit_solution(6386119942088688657)
XLA Ops:
  0.0 3.7 %convert_element_type.48 = bf16[8,262144]{1,0:T(8,128)(2,1)S(1)} convert(s32[8,262144]{1,0:T(8,128)} %param.1) | non-fusion elementwise | flops 2097152 | bytes 12582912 | tf_op jit(solution)/shard_map/convert_element_type | solution.py:42
  3.7 0.0 copy-start
  3.7 2.0 copy-done
  5.7 4.4 %collective-permute-start = (bf16[8,6144]{1,0:T(8,128)(2,1)S(1)}, bf16[8,6144]{1,0:T(8,128)(2,1)S(1)}, u32[]{:S(2)}, u32[]{:S(2)}) collective-permute-start(bf16[8,6144]{1,0:T(8,128)(2,1)S(1)} %slice.57), channel_id=1, source_target_pairs={{0,1},{2,3},{4,5},{6,7},{8,9},{10,11},{12,13},{14,15},{16,17},{18,... | collective-permute-start | bytes 294920 | tf_op jit(solution)/shard_map/ppermute | solution.py:16
  10.1 0.2 fusion.20
  10.2 34.4 %negate_convert_fusion = (bf16[1024,1,2048]{2,0,1:T(8,128)(2,1)S(1)}, bf16[1024,1,2048]{2,0,1:T(8,128)(2,1)}) fusion(), kind=kLoop, calls=%fused_computation.14 | loop fusion | flops 35651584 | bytes 8388608 | tf_op jit(solution)/shard_map/convert.1
  44.6 6.3 %pad_maximum_fusion = bf16[1024,2,2048]{2,0,1:T(8,128)(2,1)} fusion(bf16[1024,1,2048]{2,0,1:T(8,128)(2,1)S(1)} %get-tuple-element.15, bf16[1024,1,2048]{2,0,1:T(8,128)(2,1)} %get-tuple-element.16), kind=kLoop, calls=%fused_computation.11 | loop fusion | flops 4194304 | bytes 16777216 | tf_op jit(solution)/shard_map/stack | solution.py:31
  50.9 16.4 %copy.22 = bf16[1024,2,2048]{2,1,0:T(2,128)(2,1)} copy(bf16[1024,2,2048]{2,0,1:T(8,128)(2,1)} %pad_maximum_fusion) | data formatting | bytes 16777216 | tf_op jit(solution)/shard_map/stack | solution.py:31
  67.4 13.0 %reshape.100 = bf16[2048,2048,1]{1,0,2:T(8,128)(2,1)} reshape(bf16[1024,2,2048]{2,1,0:T(2,128)(2,1)} %copy.22) | data formatting | bytes 16777216 | tf_op jit(solution)/shard_map/convert_element_type | solution.py:32
  80.4 0.0 collective-permute-done
  80.4 0.0 slice-start
  80.4 3.6 %pad_maximum_fusion.1 = bf16[8,268288]{1,0:T(8,128)(2,1)S(1)} fusion(bf16[8,262144]{1,0:T(8,128)(2,1)} %copy-done, bf16[8,6144]{1,0:T(8,128)(2,1)S(1)} %collective-permute-done), kind=kLoop, calls=%fused_computation.19 | loop fusion | flops 8585216 | bytes 8585216 | tf_op jit(solution)/shard_map/concatenate | solution.py:45
  84.0 0.0 slice-start.1
  84.0 5.4 %fusion.44 = (bf16[8,128,2048]{2,0,1:T(8,128)(2,1)S(1)}, bf16[8,128,2048]{2,0,1:T(8,128)(2,1)}, bf16[8,128,2048]{2,0,1:T(8,128)(2,1)}, bf16[8,128,2048]{2,0,1:T(8,128)(2,1)}) fusion(bf16[8,131,2048]{2,0,1:T(8,128)(2,1)S(1)} %bitcast.13), kind=kLoop, calls=%fused_computation.64 | loop fusion | bytes 33554432 | tf_op jit(solution)/shard_map/slice | solution.py:48
  89.4 0.0 slice-done
  89.4 0.0 slice-done.1
  89.4 78.8 %multiply_convert_fusion = bf16[2048,8,128]{2,0,1:T(8,128)(2,1)} fusion(bf16[2048,2048,1]{1,0,2:T(8,128)(2,1)S(1)} %bitcast.17, bf16[8,128,2048]{2,0,1:T(8,128)(2,1)} %get-tuple-element.10, bf16[8,128,2048]{2,0,1:T(8,128)(2,1)} %get-tuple-element.8, bf16[8,128,2048]{2,0,1:T(8,128)(2,1)} %get-tuple-element.9, ...), kind=kOutput, calls=%fused_computation.12 | convolution fusion | flops 8619294720 | bytes 29392896 | tf_op jit(solution)/shard_map/cf,isf->cis/dot_general | solution.py:55
  168.3 6.9 %copy.27 = bf16[128,8,2,8,128]{4,2,1,3,0:T(2,128)(2,1)S(1)} copy(bf16[128,8,2,8,128]{4,2,1,0,3:T(2,128)(2,1)} %bitcast.18) | data formatting | bytes 8388608 | tf_op jit(solution)/shard_map/reshape | solution.py:57
  175.2 63.5 %all_to_all.5 = bf16[128,8,2,8,128]{4,2,1,3,0:T(2,128)(2,1)S(1)} all-to-all(bf16[128,8,2,8,128]{4,2,1,3,0:T(2,128)(2,1)S(1)} %copy.27), channel_id=1, replica_groups=mesh['gx'=64,'ta'=2] {'gx','ta'}, dimensions={0} | all-to-all | bytes 8388608 | tf_op jit(solution)/shard_map/all_to_all | solution.py:58
  238.7 3.1 %copy.28 = bf16[64,2,8,2,8,128]{5,4,1,0,3,2:T(8,128)(2,1)} copy(bf16[64,2,8,2,8,128]{5,3,2,4,1,0:T(2,128)(2,1)S(1)} %bitcast.15) | data formatting | bytes 8388608 | tf_op jit(solution)/shard_map/reshape | solution.py:59
  241.8 19.1 %fusion.46 = f32[8,1024,1024]{2,1,0:T(8,128)} fusion(bf16[8,1024,256]{2,1,0:T(8,128)(2,1)} %bitcast.14), kind=kOutput, calls=%fused_computation.66 | convolution fusion | flops 4294967296 | bytes 37748736 | tf_op jit(solution)/shard_map/dot_general | solution.py:62
  260.9 19.1 %fusion.4 = (f32[8,1,512,512]{3,2,0,1:T(8,128)}, f32[8,1,512,512]{3,2,0,1:T(8,128)}) fusion(f32[8,1024,1024]{2,1,0:T(8,128)} %fusion.46), kind=kLoop, calls=%fused_computation.10 | loop fusion | flops 4194304 | bytes 50331648 | tf_op jit(solution)/shard_map/stack | solution.py:68
  280.0 7.4 %maximum_multiply_fusion = f32[8,2,512,512]{3,2,0,1:T(8,128)S(1)} fusion(f32[8,1,512,512]{3,2,0,1:T(8,128)} %get-tuple-element.6, f32[8,1,512,512]{3,2,0,1:T(8,128)} %get-tuple-element.5), kind=kLoop, calls=%fused_computation | loop fusion | flops 8388608 | bytes 33554432 | tf_op jit(solution)/shard_map/mul | solution.py:68
  287.4 6.4 %copy.29 = f32[8,2,512,512]{3,2,1,0:T(8,128)} copy(f32[8,2,512,512]{3,2,0,1:T(8,128)S(1)} %maximum_multiply_fusion) | data formatting | bytes 33554432 | tf_op jit(solution)/shard_map/mul | solution.py:68
  (3 shorter events, 0.0 us)
Async XLA Ops:
  3.7 2.0 copy-start
  5.7 74.8 %collective-permute-start = (bf16[8,6144]{1,0:T(8,128)(2,1)S(1)}, bf16[8,6144]{1,0:T(8,128)(2,1)S(1)}, u32[]{:S(2)}, u32[]{:S(2)}) collective-permute-start(bf16[8,6144]{1,0:T(8,128)(2,1)S(1)} %slice.57), channel_id=1, source_target_pairs={{0,1},{2,3},{4,5},{6,7},{8,9},{10,11},{12,13},{14,15},{16,17},{18,... | collective-permute-start | bytes 294920 | tf_op jit(solution)/shard_map/ppermute | solution.py:16
  80.4 9.0 %slice-start = ((s8[8388608]{0:T(1024)(128)(4,1)}), s8[4194304]{0:T(1024)(128)(4,1)S(1)}, s32[]{:S(2)}) async-start(s8[8388608]{0:T(1024)(128)(4,1)} %bitcast.16), calls=%async_computation.1 | async-start | bytes 8388608
  84.0 5.4 %slice-start.1 = ((s8[8388608]{0:T(1024)(128)(4,1)}), s8[4194304]{0:T(1024)(128)(4,1)S(1)}, s32[]{:S(2)}) async-start(s8[8388608]{0:T(1024)(128)(4,1)} %bitcast.16), calls=%async_computation.2 | async-start | bytes 8388608
where the time goes:
time: 299 us; the launch traced here: 294 us
  matrix products  97.9 us (33%)
  other arithmetic  74.7 us (25%)
  blocking collectives  63.5 us (21%)
  local copies, waits for them, and re-layouts  53.2 us (18%)
  starting transfers between devices  4.37 us (1%)
    dot_general x1, matrix products, on_device(): jnp.einsum('cf,isf->cis', dft_table, filtered, preferred_element_type=jnp...  78.8 us
    all_to_all x1, blocking collectives, on_device(): lax.all_to_all(outgoing, ('gx', 'ta'), split_axis=0, concat_axis=0, tiled...  63.5 us
    another operation x1, other arithmetic  34.4 us
    another operation x1, other arithmetic, on_device(): return jnp.stack([real_part, imag_part], axis=1) * norm_factor  19.1 us
    dot_general x1, matrix products, on_device(): lax.dot_general(stacked, stacked, (((2,), (2,)), ((0,), (0,))), preferred...  19.1 us
    another operation x1, local copies, waits for them, and re-layouts, dft_rows(): rows = jnp.stack([jnp.cos(angle), -jnp.sin(angle)], axis=1)  16.4 us
    convert_element_type x1, local copies, waits for them, and re-layouts, dft_rows(): return rows.reshape(2 * chan_list.shape[0], frame_len).astype(jnp.bfloat16)  13 us
    mul x1, other arithmetic, on_device(): return jnp.stack([real_part, imag_part], axis=1) * norm_factor  7.45 us
  transfers between devices with their start and end apart: 1, of which 0 were waited for; matrix products, arithmetic and copies ran while one was open for 24% of the time, Pallas kernels for 0%

commit v1 on v0

v1 whole, which is shorter than its diff:
```python
import math

import jax
import jax.numpy as jnp
import numpy as np
from jax import lax
from jax.experimental import pallas as pl
from jax.experimental.pallas import tpu as pltpu
from jax.sharding import PartitionSpec as P

INPUTS = 512
CHAN = 1024
TAPS = 4
FRAME = 2 * CHAN
HALF = FRAME // 2
LANES = 128
TILES = FRAME // LANES
HTILES = TILES // 2
HEAD = 16
MIB = 1024 * 1024
BF16 = jnp.bfloat16
F32 = jnp.float32


def shifted(array, axis, by):
    count = lax.axis_size(axis)
    pairs = [(i, i + by) for i in range(count) if 0 <= i + by < count]
    return lax.ppermute(array, axis, pairs)


def window_rows():
    total_len = TAPS * FRAME
    positions = np.arange(total_len, dtype=np.float64)
    centred = (positions + 0.5 - total_len / 2.0) / FRAME
    hamming = 0.54 - 0.46 * np.cos(2.0 * np.pi * positions / (total_len - 1))
    return (np.sinc(centred) * hamming).astype(np.float32).reshape(TAPS * TILES, LANES)


def dft_half(parity):
    chan = 2 * np.arange(CHAN // 2) + parity
    phase = chan[:, None] * np.arange(HALF)[None, :] % FRAME
    angle = phase * (2.0 * np.pi / FRAME)
    rows = np.stack([np.cos(angle), -np.sin(angle)], axis=1)
    return rows.reshape(CHAN, HALF).astype(BF16)


def taps_into(acc_ref, history, frame_at, weights, count, base=0):
    def step(block, carry):
        carry = list(carry)
        for inner in range(8):
            s = block * 8 + inner
            new = frame_at(s)
            total = weights[0] * carry[0] + weights[1] * carry[1]
            total = total + weights[2] * carry[2] + weights[3] * new
            acc_ref[pl.ds(pl.multiple_of(s * 8, 8), 8), :] = total
            carry = [carry[1], carry[2], new]
        return tuple(carry)

    lax.fori_loop(0, count // 8, step, tuple(history))


def fold_into(fe_ref, fo_ref, lo_ref, hi_ref, spec_here, count, column, inputs_here):
    lanes = pl.ds(pl.multiple_of(column * LANES, LANES), LANES)
    for i in range(inputs_here):
        for c in range(count // 16):
            rows = pl.ds(c * 16 * inputs_here + i, 16, stride=inputs_here)
            low = lo_ref[rows, :].astype(BF16)
            high = hi_ref[rows, :].astype(BF16)
            place = pl.ds(i * spec_here + c * 16, 16)
            fe_ref[place, lanes] = low + high
            fo_ref[place, lanes] = low - high


def window_at(w_ref, tile):
    return [jnp.broadcast_to(w_ref[pl.ds(t * TILES + tile, 1), :], (8, LANES)) for t in range(TAPS)]


def filter_kernel(spec_here, v_hbm, w_ref, fe_ref, fo_ref, lo_acc, hi_acc):
    def body(lo_ref, hi_ref):
        j = pl.program_id(0)
        for ref, acc, tile in ((lo_ref, lo_acc, j), (hi_ref, hi_acc, j + HTILES)):
            weights = window_at(w_ref, tile)
            zero = jnp.zeros((8, LANES), F32)
            taps_into(acc, [zero] * 3, lambda s: ref[s, 0].astype(F32), weights, spec_here)
        fold_into(fe_ref, fo_ref, lo_acc, hi_acc, spec_here, spec_here, j, 8)

    block = (spec_here, 1, 8, LANES)
    pltpu.emit_pipeline(
        body,
        grid=(HTILES,),
        in_specs=[
            pl.BlockSpec(block, lambda j: (0, j, 0, 0)),
            pl.BlockSpec(block, lambda j: (0, j + HTILES, 0, 0)),
        ],
        out_specs=[],
    )(v_hbm, v_hbm)


def dft_kernel(spec_here, head_ref, halo_ref, w_ref, te_ref, to_ref, fe_in, fo_in, out_ref, fe_ref, fo_ref, lo_acc, hi_acc, scr):
    def first(j, carry):
        for acc, tile in ((lo_acc, j), (hi_acc, j + HTILES)):
            weights = window_at(w_ref, tile)
            history = [halo_ref[t, tile].astype(F32) for t in range(TAPS - 1)]
            taps_into(acc, history, lambda s: head_ref[s, tile].astype(F32), weights, HEAD)
        fold_into(fe_ref, fo_ref, lo_acc, hi_acc, spec_here, HEAD, j, 8)
        return carry

    lax.fori_loop(0, HTILES, first, 0)
    scale = 1.0 / (64.0 * math.sqrt(FRAME))
    for parity, (table, data) in enumerate(((te_ref, fe_ref), (to_ref, fo_ref))):

        def pair(ip, carry):
            rhs = data[pl.ds(pl.multiple_of(ip * 2 * spec_here, 2 * spec_here), 2 * spec_here), :]
            for rc in range(2):
                lhs = table[rc * 512 : (rc + 1) * 512, :]
                acc = lax.dot_general(lhs, rhs, (((1,), (1,)), ((), ())), preferred_element_type=F32) * scale
                for side in range(2):
                    rows = pl.ds(rc * 512 * 8 + ip * 2 + side, 512, stride=8)
                    scr[rows, :] = acc[:, side * spec_here : (side + 1) * spec_here]
            return carry

        lax.fori_loop(0, 4, pair, 0)

        def emit(d, carry):
            rows = scr[pl.ds(pl.multiple_of(d * 256, 256), 256), :].astype(BF16)
            out_ref[pl.ds(d * 4, 4), pl.ds(parity * 64, 64), :] = rows.reshape(4, 64, LANES)
            return carry

        lax.fori_loop(0, 32, emit, 0)


def gram_kernel(norm, got_ref, out_hbm, mat):
    def body(out_ref):
        k = pl.program_id(0)
        row = pl.multiple_of((k % 2) * 64 + (k // 2) * 16, 16)
        for ta in range(2):
            tile = got_ref[:, ta, pl.ds(row, 16), :].astype(F32).reshape(64, 2, 8, LANES)
            real = tile[:, 0].reshape(INPUTS, LANES)
            imag = tile[:, 1].reshape(INPUTS, LANES)
            mat[:INPUTS, ta * 128 : (ta + 1) * 128] = real.astype(BF16)
            mat[:INPUTS, 256 + ta * 128 : 256 + (ta + 1) * 128] = imag.astype(BF16)
            mat[INPUTS:, ta * 128 : (ta + 1) * 128] = imag.astype(BF16)
            mat[INPUTS:, 256 + ta * 128 : 256 + (ta + 1) * 128] = (-real).astype(BF16)
        right = mat[:INPUTS, :]
        for p in range(2):
            left = mat[p * INPUTS : (p + 1) * INPUTS, :]
            gram = lax.dot_general(left, right, (((1,), (1,)), ((), ())), preferred_element_type=F32)
            out_ref[0, p] = gram * norm

    pltpu.emit_pipeline(
        body,
        grid=(8,),
        in_specs=[],
        out_specs=[pl.BlockSpec((1, 2, INPUTS, INPUTS), lambda k: (k, 0, 0, 0))],
    )(out_hbm)


VMEM = pl.BlockSpec(memory_space=pltpu.VMEM)
ANY = pl.BlockSpec(memory_space=pl.ANY)


def filter_call(frames, window):
    spec_here = frames.shape[0]
    rows = 8 * spec_here
    folded = jax.ShapeDtypeStruct((rows, HALF), BF16)
    return pl.pallas_call(
        lambda *refs: filter_kernel(spec_here, *refs),
        out_shape=(folded, folded),
        in_specs=[ANY, VMEM],
        out_specs=(VMEM, VMEM),
        scratch_shapes=[pltpu.VMEM((rows, LANES), F32)] * 2,
        compiler_params=pltpu.CompilerParams(vmem_limit_bytes=20 * MIB),
        cost_estimate=pl.CostEstimate(flops=8 * 2 * 1024 * 1024, bytes_accessed=8 * MIB, transcendentals=0),
        name="filter",
    )(frames, window)


def dft_call(head, halo, window, table_even, table_odd, even, odd):
    rows = even.shape[0]
    spec_here = rows // 8
    folded = jax.ShapeDtypeStruct((rows, HALF), BF16)
    return pl.pallas_call(
        lambda *refs: dft_kernel(spec_here, *refs),
        out_shape=(jax.ShapeDtypeStruct((128, 128, spec_here), BF16), folded, folded),
        in_specs=[VMEM] * 7,
        out_specs=(VMEM, VMEM, VMEM),
        input_output_aliases={5: 1, 6: 2},
        scratch_shapes=[pltpu.VMEM((HEAD * 8, LANES), F32)] * 2 + [pltpu.VMEM((8 * CHAN, spec_here), F32)],
        compiler_params=pltpu.CompilerParams(vmem_limit_bytes=40 * MIB),
        cost_estimate=pl.CostEstimate(flops=4 * 1024**3, bytes_accessed=12 * MIB, transcendentals=0),
        name="dft",
    )(head, halo, window, table_even, table_odd, even, odd)[0]


def gram_call(arrived, norm):
    return pl.pallas_call(
        lambda *refs: gram_kernel(norm, *refs),
        out_shape=jax.ShapeDtypeStruct((8, 2, INPUTS, INPUTS), F32),
        in_specs=[VMEM],
        out_specs=ANY,
        scratch_shapes=[pltpu.VMEM((2 * INPUTS, 512), BF16)],
        compiler_params=pltpu.CompilerParams(vmem_limit_bytes=20 * MIB),
        cost_estimate=pl.CostEstimate(flops=4 * 1024**3, bytes_accessed=20 * MIB, transcendentals=0),
        name="gram",
    )(arrived)


def on_device(voltages):
    inputs_here, total_len = voltages.shape
    spec_here = total_len // FRAME
    frames = voltages.reshape(inputs_here, spec_here, TILES, LANES).transpose(1, 2, 0, 3)
    tail = frames[spec_here - (TAPS - 1) :].astype(BF16)
    halo = shifted(tail, "ta", 1)
    window = jnp.asarray(window_rows())
    even, odd = filter_call(frames, window)
    table_even, table_odd = jnp.asarray(dft_half(0)), jnp.asarray(dft_half(1))
    outgoing = dft_call(frames[:HEAD], halo, window, table_even, table_odd, even, odd)
    arrived = lax.all_to_all(outgoing, ("gx", "ta"), split_axis=0, concat_axis=0, tiled=True)
    norm = 1.0 / math.sqrt(2 * spec_here)
    return gram_call(arrived.reshape(64, 2, 128, spec_here), norm)


def solution(mesh):
    placed = (P("gx", "ta"),)
    return jax.shard_map(
        on_device,
        mesh=mesh,
        in_specs=placed,
        out_specs=P(("gx", "ta"), None, None, None),
        check_vma=False,
    )
```

time: 299 us -> 97.4 us (0.33); the launches traced: 294 us -> 97.2 us
  matrix products: 97.9 us -> 0 us
  other arithmetic: 74.7 us -> 0.95 us
  local copies, waits for them, and re-layouts: 53.2 us -> 4.71 us
  Pallas kernels: 0 us -> 23.8 us
    dot_general x2 -> x0, matrix products: 97.9 us -> none  [the longest x1 78.8 us: on_device(): jnp.einsum('cf,isf->cis', dft_table, filtered, preferred_element_type=jnp...]
    another operation x3 -> x1, other arithmetic: 59.8 us -> 0.95 us
    pallas_call x0 -> x3, Pallas kernels: none -> 23.8 us  [the longest x1 9.39 us: gram_call(): pl.pallas_call(lambda *refs: gram_kernel(norm, *refs), out_shape=jax.Shap...]
    another operation x1 -> x0, local copies, waits for them, and re-layouts: 16.4 us -> none  [dft_rows(): rows = jnp.stack([jnp.cos(angle), -jnp.sin(angle)], axis=1)]
    convert_element_type x1 -> x0, local copies, waits for them, and re-layouts: 13 us -> none  [dft_rows(): return rows.reshape(2 * chan_list.shape[0], frame_len).astype(jnp.bfloat16)]
    reshape x2 -> x0, local copies, waits for them, and re-layouts: 10 us -> none  [the longest x1 6.91 us: on_device(): spectra.reshape(gx_count * ta_count, per_dev, 2, inputs_here, spec_here)]
    mul x2 -> x0, other arithmetic: 7.62 us -> none  [the longest x1 7.45 us: on_device(): return jnp.stack([real_part, imag_part], axis=1) * norm_factor]
    mul x1 -> x0, local copies, waits for them, and re-layouts: 6.38 us -> none  [on_device(): return jnp.stack([real_part, imag_part], axis=1) * norm_factor]
  transfers between devices with their start and end apart: 1 -> 1, of which waited for: 0 -> 0; matrix products, arithmetic and copies ran while one was open for 24% -> 1% of each run, Pallas kernels for 0% -> 7%
where the time goes in v1:
time: 97.4 us; the launch traced here: 97.2 us
  blocking collectives  63.3 us (65%)
  Pallas kernels  23.8 us (24%)
  local copies, waits for them, and re-layouts  4.71 us (5%)
  starting transfers between devices  4.38 us (4%)
    all_to_all x1, blocking collectives, on_device(): lax.all_to_all(outgoing, ('gx', 'ta'), split_axis=0, concat_axis=0, tiled...  63.3 us
    pallas_call x1, Pallas kernels, gram_call(): pl.pallas_call(lambda *refs: gram_kernel(norm, *refs), out_shape=jax.Shap...  9.39 us
    pallas_call x1, Pallas kernels, dft_call(): pl.pallas_call(lambda *refs: dft_kernel(spec_here, *refs), out_shape=(jax...  7.87 us
    pallas_call x1, Pallas kernels, filter_call(): pl.pallas_call(lambda *refs: filter_kernel(spec_here, *refs), out_shape=(...  6.55 us
    ppermute x1, starting transfers between devices, shifted(): return lax.ppermute(array, axis, pairs)  4.38 us
    unnamed x8, local copies, waits for them, and re-layouts  3.39 us
  transfers between devices with their start and end apart: 1, of which 0 were waited for; matrix products, arithmetic and copies ran while one was open for 1% of the time, Pallas kernels for 7%

profile of v1, /device:TPU:1, one launch (start us, length us, event | category | flops | bytes accessed | tf_op | source)
XLA Modules:
  0.0 97.2 jit_solution(8953069225108020300)
XLA Ops:
  0.0 0.0 copy-start.1
  0.0 0.9 slice_convert_fusion
  1.0 4.4 %collective-permute-start = (bf16[3,16,8,128]{3,2,1,0:T(8,128)(2,1)S(1)}, bf16[3,16,8,128]{3,2,1,0:T(8,128)(2,1)S(1)}, u32[]{:S(2)}, u32[]{:S(2)}) collective-permute-start(bf16[3,16,8,128]{3,2,1,0:T(8,128)(2,1)S(1)} %slice_convert_fusion), channel_id=1, source_target_pairs={{0,1},{2,3},{4,5},{6,7},{8,9},{10,11},{12,13},{14,15},{16,17},{18,... | collective-permute-start | bytes 294920 | tf_op jit(solution)/shard_map/ppermute | solution.py:28
  5.3 1.3 %slice.9.refs_0_ = s32[16,16,8,128]{3,2,1,0:T(8,128)S(1)} slice(s32[128,16,8,128]{3,2,1,0:T(8,128)} %bitcast.6), slice={[0:16], [0:16], [0:8], [0:128]} | slice | bytes 2097152 | tf_op jit(solution)/shard_map/slice | solution.py:217
  6.7 0.0 copy-done.1
  6.7 0.0 copy-start
  6.7 3.4 %copy-done = s32[8,262144]{1,0:T(8,128)S(1)} copy-done((s32[8,262144]{1,0:T(8,128)S(1)}, s32[8,262144]{1,0:T(8,128)}, u32[]{:S(2)}) %copy-start) | copy-done | bytes 8388632
  10.1 0.0 copy-start.2
  10.1 0.0 copy-start.3
  10.1 6.5 %filter.1 = (bf16[1024,1024]{1,0:T(8,128)(2,1)S(1)}, bf16[1024,1024]{1,0:T(8,128)(2,1)S(1)}) custom-call(s32[128,16,8,128]{3,2,1,0:T(8,128)S(1)} %bitcast.7, f32[64,128]{1,0:T(8,128)S(1)} %copy-done.1), custom_call_target="tpu_custom_call" | custom-call | flops 16777216 | bytes 8388608 | tf_op jit(solution)/shard_map/filter/pallas_call | solution.py:166
  16.6 0.0 collective-permute-done.refs_1_
  16.6 0.0 copy-done.2
  16.6 0.0 copy-done.3
  16.7 7.9 %dft.1 = (bf16[128,128,128]{2,1,0:T(8,128)(2,1)S(1)}, bf16[1024,1024]{1,0:T(8,128)(2,1)S(1)}, bf16[1024,1024]{1,0:T(8,128)(2,1)S(1)}) custom-call(s32[16,16,8,128]{3,2,1,0:T(8,128)S(1)} %slice.9.refs_0_, bf16[3,16,8,128]{3,2,1,0:T(8,128)(2,1)S(1)} %collective-permute-done.refs_1_, ...), custom_call_target="tpu_custom_call", output_to_operand_aliasing={{1}: (5, {}), {2}: (6, {})} | custom-call | flops 4294967296 | bytes 12582912 | tf_op jit(solution)/shard_map/dft/pallas_call | solution.py:182
  24.5 63.3 %all_to_all.5 = bf16[128,128,128]{2,1,0:T(8,128)(2,1)S(1)} all-to-all(bf16[128,128,128]{2,1,0:T(8,128)(2,1)S(1)} %get-tuple-element.10), channel_id=1, replica_groups=mesh['gx'=64,'ta'=2] {'gx','ta'}, dimensions={0} | all-to-all | bytes 8388608 | tf_op jit(solution)/shard_map/all_to_all | solution.py:218
  87.8 9.4 %gram.1 = f32[8,2,512,512]{3,2,1,0:T(8,128)} custom-call(bf16[64,2,128,128]{3,2,1,0:T(8,128)(2,1)S(1)} %bitcast.4), custom_call_target="tpu_custom_call" | custom-call | flops 4294967296 | bytes 20971520 | tf_op jit(solution)/shard_map/gram/pallas_call | solution.py:196
Async XLA Ops:
  0.0 6.7 %copy-start.1 = (f32[64,128]{1,0:T(8,128)S(1)}, f32[64,128]{1,0:T(8,128)}, u32[]{:S(2)}) copy-start(f32[64,128]{1,0:T(8,128)} %constant.6.clone.refs_1_.refs_2_) | copy-start | bytes 98308
  1.0 15.7 %collective-permute-start = (bf16[3,16,8,128]{3,2,1,0:T(8,128)(2,1)S(1)}, bf16[3,16,8,128]{3,2,1,0:T(8,128)(2,1)S(1)}, u32[]{:S(2)}, u32[]{:S(2)}) collective-permute-start(bf16[3,16,8,128]{3,2,1,0:T(8,128)(2,1)S(1)} %slice_convert_fusion), channel_id=1, source_target_pairs={{0,1},{2,3},{4,5},{6,7},{8,9},{10,11},{12,13},{14,15},{16,17},{18,... | collective-permute-start | bytes 294920 | tf_op jit(solution)/shard_map/ppermute | solution.py:28
  6.7 3.4 %copy-start = (s32[8,262144]{1,0:T(8,128)S(1)}, s32[8,262144]{1,0:T(8,128)}, u32[]{:S(2)}) copy-start(s32[8,262144]{1,0:T(8,128)} %param.4) | copy-start | bytes 25165828
  10.1 6.6 %copy-start.2 = (bf16[1024,1024]{1,0:T(8,128)(2,1)S(1)}, bf16[1024,1024]{1,0:T(8,128)(2,1)}, u32[]{:S(2)}) copy-start(bf16[1024,1024]{1,0:T(8,128)(2,1)} %constant.8.clone.refs_4_) | copy-start | bytes 6291460
  10.1 6.6 %copy-start.3 = (bf16[1024,1024]{1,0:T(8,128)(2,1)S(1)}, bf16[1024,1024]{1,0:T(8,128)(2,1)}, u32[]{:S(2)}) copy-start(bf16[1024,1024]{1,0:T(8,128)(2,1)} %constant.7.clone.refs_3_) | copy-start | bytes 6291460

commit v2 on v0

v2 whole, which is shorter than its diff:
```python
import math

import jax
import jax.numpy as jnp
import numpy as np
from jax import lax
from jax.experimental import pallas as pl
from jax.experimental.pallas import tpu as pltpu
from jax.sharding import PartitionSpec as P

INPUTS = 512
CHAN = 1024
TAPS = 4
FRAME = 2 * CHAN
LANES = 128
TILES = FRAME // LANES
BLOCK = 16
MIB = 1024 * 1024
BF16 = jnp.bfloat16
F32 = jnp.float32


def shifted(array, axis, by):
    count = lax.axis_size(axis)
    pairs = [(i, i + by) for i in range(count) if 0 <= i + by < count]
    return lax.ppermute(array, axis, pairs)


def window_rows():
    total_len = TAPS * FRAME
    positions = np.arange(total_len, dtype=np.float64)
    centred = (positions + 0.5 - total_len / 2.0) / FRAME
    hamming = 0.54 - 0.46 * np.cos(2.0 * np.pi * positions / (total_len - 1))
    return (np.sinc(centred) * hamming).astype(np.float32).reshape(TAPS * TILES, LANES)


def dft_rows(first, step, length):
    chan = np.arange(first, CHAN, step)
    phase = chan[:, None] * np.arange(length)[None, :] % FRAME
    angle = phase * (2.0 * np.pi / FRAME)
    rows = np.stack([np.cos(angle), -np.sin(angle)], axis=1)
    return rows.reshape(2 * chan.size, length).astype(BF16)


def filter_block(frame_at, w_ref, acc_ref, f_ref, column, block, spec_here):
    for q in range(4):
        tile = column + 4 * q
        weights = [jnp.broadcast_to(w_ref[pl.ds(t * TILES + tile, 1), :], (8, LANES)) for t in range(TAPS)]
        frames = [frame_at(f, tile).astype(F32) for f in range(BLOCK + TAPS - 1)]
        for s in range(BLOCK):
            total = weights[0] * frames[s] + weights[1] * frames[s + 1]
            total = total + weights[2] * frames[s + 2] + weights[3] * frames[s + 3]
            acc_ref[q, s * 8 : (s + 1) * 8, :] = total
    for i in range(8):
        parts = [acc_ref[q, pl.ds(i, BLOCK, stride=8), :].astype(BF16) for q in range(4)]
        wide = [part.astype(F32) for part in parts]
        evens, odds = wide[0] + wide[2], wide[1] + wide[3]
        rows = pl.ds(pl.multiple_of(i * spec_here + block * BLOCK, BLOCK), BLOCK)
        f_ref[column, rows, :] = (evens + odds).astype(BF16)
        f_ref[4 + column, rows, :] = (evens - odds).astype(BF16)
        f_ref[8 + column, rows, :] = parts[0] - parts[2]
        f_ref[12 + column, rows, :] = parts[1] - parts[3]


def filter_kernel(spec_here, v_hbm, w_hbm, f_ref, head_ref, w_ref, frames, acc, sems, side_sems):
    blocks = spec_here // BLOCK

    def fetch(b):
        part = pl.ds(b * BLOCK, BLOCK)
        return pltpu.make_async_copy(v_hbm.at[part], frames.at[part], sems.at[b])

    window = pltpu.make_async_copy(w_hbm, w_ref, side_sems.at[0])
    window.start()
    for b in range(blocks):
        fetch(b).start()
    head = pltpu.make_async_copy(v_hbm.at[pl.ds(0, BLOCK)], head_ref, side_sems.at[1])
    head.start()
    window.wait()
    fetch(0).wait()

    def step(b, carry):
        fetch(b).wait()

        def columns(column, carry):
            filter_block(
                lambda f, tile: frames[b * BLOCK - (TAPS - 1) + f, tile], w_ref, acc, f_ref, column, b, spec_here
            )
            return carry

        return lax.fori_loop(0, 4, columns, carry)

    lax.fori_loop(1, blocks, step, 0)
    head.wait()


def dft_kernel(spec_here, head_ref, halo_ref, w_ref, t0_ref, t1_ref, t2_ref, f_in, out_ref, f_ref, acc, scr):
    def first(column, carry):
        def frame_at(f, tile):
            return halo_ref[f, tile] if f < TAPS - 1 else head_ref[f - (TAPS - 1), tile]

        filter_block(frame_at, w_ref, acc, f_ref, column, 0, spec_here)
        return carry

    lax.fori_loop(0, 4, first, 0)
    scale = 1.0 / (64.0 * math.sqrt(FRAME))
    pair = 2 * spec_here
    groups = ((t0_ref, 0, 0, 0, 32), (t1_ref, 4, 4096, 32, 32), (t2_ref, 8, 8192, 64, 64))
    for table, column, base, place, each in groups:
        rows_all, length = table.shape
        for ip in range(4):
            right = jnp.concatenate(
                [f_ref[column + c, ip * pair : (ip + 1) * pair, :] for c in range(length // LANES)], axis=1
            )
            for part in range(rows_all // 512):
                left = table[part * 512 : (part + 1) * 512, :]
                sums = lax.dot_general(left, right, (((1,), (1,)), ((), ())), preferred_element_type=F32) * scale
                for side in range(2):
                    rows = pl.ds(base + part * 4096 + ip * 2 + side, 512, stride=8)
                    scr[rows, :] = sums[:, side * spec_here : (side + 1) * spec_here]
        for d in range(0, 128, 4):
            rows = scr[base + d * each : base + (d + 4) * each, :].astype(BF16)
            out_ref[d : d + 4, place : place + each, :] = rows.reshape(4, each, LANES)


def gram_kernel(norm, got_ref, out_hbm, mats, out, sems):
    def copy_out(k, p):
        return pltpu.make_async_copy(out.at[k, p], out_hbm.at[k, p], sems.at[k, p])

    def channel(k, row, mat):
        for ta in range(2):
            tile = got_ref[:, ta, pl.ds(pl.multiple_of(row, 16), 16), :].astype(F32).reshape(64, 2, 8, LANES)
            real = tile[:, 0].reshape(INPUTS, LANES).astype(BF16)
            imag = tile[:, 1].reshape(INPUTS, LANES).astype(BF16)
            mat[:INPUTS, ta * 128 : (ta + 1) * 128] = real
            mat[:INPUTS, 256 + ta * 128 : 256 + (ta + 1) * 128] = imag
            mat[INPUTS:, ta * 128 : (ta + 1) * 128] = imag
            mat[INPUTS:, 256 + ta * 128 : 256 + (ta + 1) * 128] = -real
        for p in range(2):
            left = mat[p * INPUTS : (p + 1) * INPUTS, :]
            gram = lax.dot_general(left, mat[:INPUTS, :], (((1,), (1,)), ((), ())), preferred_element_type=F32)
            out[k, p] = gram * norm
            copy_out(k, p).start()

    def step(b, carry):
        channel(2 * b, (b % 2) * 32 + (b // 2) * 16, mats.at[0])
        channel(2 * b + 1, 64 + b * 16, mats.at[1])
        return carry

    lax.fori_loop(0, 4, step, 0)
    for k in range(8):
        for p in range(2):
            copy_out(k, p).wait()


VMEM = pl.BlockSpec(memory_space=pltpu.VMEM)
ANY = pl.BlockSpec(memory_space=pl.ANY)


def filter_call(frames, window):
    spec_here = frames.shape[0]
    return pl.pallas_call(
        lambda *refs: filter_kernel(spec_here, *refs),
        out_shape=(
            jax.ShapeDtypeStruct((TILES, 8 * spec_here, LANES), BF16),
            jax.ShapeDtypeStruct((BLOCK, TILES, 8, LANES), jnp.int32),
            window,
        ),
        in_specs=[ANY, ANY],
        out_specs=(VMEM, VMEM, VMEM),
        scratch_shapes=[
            pltpu.VMEM((spec_here, TILES, 8, LANES), jnp.int32),
            pltpu.VMEM((4, BLOCK * 8, LANES), F32),
            pltpu.SemaphoreType.DMA((spec_here // BLOCK,)),
            pltpu.SemaphoreType.DMA((2,)),
        ],
        compiler_params=pltpu.CompilerParams(vmem_limit_bytes=46 * MIB),
        cost_estimate=pl.CostEstimate(flops=8 * 2 * 1024 * 1024, bytes_accessed=8 * MIB, transcendentals=0),
        name="filter",
    )(frames, window)


def dft_call(head, halo, window, tables, folded):
    spec_here = folded.shape[1] // 8
    return pl.pallas_call(
        lambda *refs: dft_kernel(spec_here, *refs),
        out_shape=(jax.ShapeDtypeStruct((128, 128, spec_here), BF16), folded),
        in_specs=[VMEM] * 7,
        out_specs=(VMEM, VMEM),
        input_output_aliases={6: 1},
        scratch_shapes=[pltpu.VMEM((4, BLOCK * 8, LANES), F32), pltpu.VMEM((8 * FRAME, spec_here), F32)],
        compiler_params=pltpu.CompilerParams(vmem_limit_bytes=40 * MIB),
        cost_estimate=pl.CostEstimate(flops=3 * 1024**3, bytes_accessed=12 * MIB, transcendentals=0),
        name="dft",
    )(head, halo, window, *tables, folded)[0]


def gram_call(arrived, norm):
    return pl.pallas_call(
        lambda *refs: gram_kernel(norm, *refs),
        out_shape=jax.ShapeDtypeStruct((8, 2, INPUTS, INPUTS), F32),
        in_specs=[VMEM],
        out_specs=ANY,
        scratch_shapes=[
            pltpu.VMEM((2, 2 * INPUTS, 512), BF16),
            pltpu.VMEM((8, 2, INPUTS, INPUTS), F32),
            pltpu.SemaphoreType.DMA((8, 2)),
        ],
        compiler_params=pltpu.CompilerParams(vmem_limit_bytes=40 * MIB),
        cost_estimate=pl.CostEstimate(flops=4 * 1024**3, bytes_accessed=20 * MIB, transcendentals=0),
        name="gram",
    )(arrived)


def on_device(voltages):
    inputs_here, total_len = voltages.shape
    spec_here = total_len // FRAME
    frames = voltages.reshape(inputs_here, spec_here, TILES, LANES).transpose(1, 2, 0, 3)
    tail = frames[spec_here - (TAPS - 1) :].astype(BF16)
    halo = shifted(tail, "ta", 1)
    window = jnp.asarray(window_rows())
    folded, head, window = filter_call(frames, window)
    tables = [jnp.asarray(dft_rows(0, 4, 512)), jnp.asarray(dft_rows(2, 4, 512)), jnp.asarray(dft_rows(1, 2, 1024))]
    outgoing = dft_call(head, halo, window, tables, folded)
    arrived = lax.all_to_all(outgoing, ("gx", "ta"), split_axis=0, concat_axis=0, tiled=True)
    norm = 1.0 / math.sqrt(2 * spec_here)
    return gram_call(arrived.reshape(64, 2, 128, spec_here), norm)


def solution(mesh):
    placed = (P("gx", "ta"),)
    return jax.shard_map(
        on_device,
        mesh=mesh,
        in_specs=placed,
        out_specs=P(("gx", "ta"), None, None, None),
        check_vma=False,
    )
```

time: 299 us -> 86.6 us (0.29); the launches traced: 294 us -> 86.3 us
  matrix products: 97.9 us -> 0 us
  other arithmetic: 74.7 us -> 0.94 us
  local copies, waits for them, and re-layouts: 53.2 us -> 0.76 us
  Pallas kernels: 0 us -> 16.9 us
    dot_general x2 -> x0, matrix products: 97.9 us -> none  [the longest x1 78.8 us: on_device(): jnp.einsum('cf,isf->cis', dft_table, filtered, preferred_element_type=jnp...]
    another operation x3 -> x1, other arithmetic: 59.8 us -> 0.94 us
    pallas_call x0 -> x3, Pallas kernels: none -> 16.9 us  [the longest x1 6.79 us: gram_call(): pl.pallas_call(lambda *refs: gram_kernel(norm, *refs), out_shape=jax.Shap...]
    another operation x1 -> x0, local copies, waits for them, and re-layouts: 16.4 us -> none  [dft_rows(): rows = jnp.stack([jnp.cos(angle), -jnp.sin(angle)], axis=1)]
    convert_element_type x1 -> x0, local copies, waits for them, and re-layouts: 13 us -> none  [dft_rows(): return rows.reshape(2 * chan_list.shape[0], frame_len).astype(jnp.bfloat16)]
    reshape x2 -> x0, local copies, waits for them, and re-layouts: 10 us -> none  [the longest x1 6.91 us: on_device(): spectra.reshape(gx_count * ta_count, per_dev, 2, inputs_here, spec_here)]
    mul x2 -> x0, other arithmetic: 7.62 us -> none  [the longest x1 7.45 us: on_device(): return jnp.stack([real_part, imag_part], axis=1) * norm_factor]
    mul x1 -> x0, local copies, waits for them, and re-layouts: 6.38 us -> none  [on_device(): return jnp.stack([real_part, imag_part], axis=1) * norm_factor]
  transfers between devices with their start and end apart: 1 -> 1, of which waited for: 0 -> 0; matrix products, arithmetic and copies ran while one was open for 24% -> 0% of each run, Pallas kernels for 0% -> 6%
where the time goes in v2:
time: 86.6 us; the launch traced here: 86.3 us
  blocking collectives  63.3 us (73%)
  Pallas kernels  16.9 us (20%)
  starting transfers between devices  4.38 us (5%)
  other arithmetic  0.94 us (1%)
    all_to_all x1, blocking collectives, on_device(): lax.all_to_all(outgoing, ('gx', 'ta'), split_axis=0, concat_axis=0, tiled...  63.3 us
    pallas_call x1, Pallas kernels, gram_call(): pl.pallas_call(lambda *refs: gram_kernel(norm, *refs), out_shape=jax.Shap...  6.79 us
    pallas_call x1, Pallas kernels, filter_call(): pl.pallas_call(lambda *refs: filter_kernel(spec_here, *refs), out_shape=(...  5.3 us
    pallas_call x1, Pallas kernels, dft_call(): pl.pallas_call(lambda *refs: dft_kernel(spec_here, *refs), out_shape=(jax...  4.83 us
    ppermute x1, starting transfers between devices, shifted(): return lax.ppermute(array, axis, pairs)  4.38 us
  transfers between devices with their start and end apart: 1, of which 0 were waited for; matrix products, arithmetic and copies ran while one was open for 0% of the time, Pallas kernels for 6%

profile of v2, /device:TPU:1, one launch (start us, length us, event | category | flops | bytes accessed | tf_op | source)
XLA Modules:
  0.0 86.3 jit_solution(10093517947995549962)
XLA Ops:
  0.0 0.9 %slice_convert_fusion = bf16[3,16,8,128]{3,2,1,0:T(8,128)(2,1)S(1)} fusion(s32[128,16,8,128]{3,2,1,0:T(8,128)} %bitcast.5), kind=kLoop, calls=%fused_computation | loop fusion | flops 49152 | bytes 294912 | tf_op jit(solution)/shard_map/convert
  0.9 4.4 %collective-permute-start = (bf16[3,16,8,128]{3,2,1,0:T(8,128)(2,1)S(1)}, bf16[3,16,8,128]{3,2,1,0:T(8,128)(2,1)S(1)}, u32[]{:S(2)}, u32[]{:S(2)}) collective-permute-start(bf16[3,16,8,128]{3,2,1,0:T(8,128)(2,1)S(1)} %slice_convert_fusion), channel_id=1, source_target_pairs={{0,1},{2,3},{4,5},{6,7},{8,9},{10,11},{12,13},{14,15},{16,17},{18,... | collective-permute-start | bytes 294920 | tf_op jit(solution)/shard_map/ppermute | solution.py:26
  5.3 0.0 copy-start
  5.3 0.7 copy-done
  6.1 0.0 copy-start.1
  6.1 0.0 copy-start.2
  6.1 0.0 copy-start.3
  6.1 5.3 %filter.1 = (bf16[16,1024,128]{2,1,0:T(8,128)(2,1)S(1)}, s32[16,16,8,128]{3,2,1,0:T(8,128)S(1)}, f32[64,128]{1,0:T(8,128)S(1)}) custom-call(s32[128,16,8,128]{3,2,1,0:T(8,128)} %bitcast.6, f32[64,128]{1,0:T(8,128)S(1)} %copy-done), custom_call_target="tpu_custom_call" | custom-call | flops 16777216 | bytes 8388608 | tf_op jit(solution)/shard_map/filter/pallas_call | solution.py:161
  11.4 0.0 collective-permute-done.refs_1_
  11.4 0.0 copy-done.1
  11.4 0.0 copy-done.2
  11.4 0.0 copy-done.3
  11.4 4.8 %dft.1 = (bf16[128,128,128]{2,1,0:T(8,128)(2,1)S(1)}, bf16[16,1024,128]{2,1,0:T(8,128)(2,1)S(1)}) custom-call(s32[16,16,8,128]{3,2,1,0:T(8,128)S(1)} %get-tuple-element.9.refs_0_, bf16[3,16,8,128]{3,2,1,0:T(8,128)(2,1)S(1)} %collective-permute-done.refs_1_, f32[64,128]{1,0:T(8,128)S(1)} %get-tuple-element.10.refs_2_, ...), custom_call_target="tpu_custom_call", output_to_operand_aliasing={{1}: (6, {})} | custom-call | flops 3221225472 | bytes 12582912 | tf_op jit(solution)/shard_map/dft/pallas_call | solution.py:184
  16.3 63.3 %all_to_all.5 = bf16[128,128,128]{2,1,0:T(8,128)(2,1)S(1)} all-to-all(bf16[128,128,128]{2,1,0:T(8,128)(2,1)S(1)} %get-tuple-element.12), channel_id=1, replica_groups=mesh['gx'=64,'ta'=2] {'gx','ta'}, dimensions={0} | all-to-all | bytes 8388608 | tf_op jit(solution)/shard_map/all_to_all | solution.py:224
  79.5 6.8 %gram.1 = f32[8,2,512,512]{3,2,1,0:T(8,128)} custom-call(bf16[64,2,128,128]{3,2,1,0:T(8,128)(2,1)S(1)} %bitcast.4), custom_call_target="tpu_custom_call" | custom-call | flops 4294967296 | bytes 20971520 | tf_op jit(solution)/shard_map/gram/pallas_call | solution.py:198
Async XLA Ops:
  0.9 10.5 %collective-permute-start = (bf16[3,16,8,128]{3,2,1,0:T(8,128)(2,1)S(1)}, bf16[3,16,8,128]{3,2,1,0:T(8,128)(2,1)S(1)}, u32[]{:S(2)}, u32[]{:S(2)}) collective-permute-start(bf16[3,16,8,128]{3,2,1,0:T(8,128)(2,1)S(1)} %slice_convert_fusion), channel_id=1, source_target_pairs={{0,1},{2,3},{4,5},{6,7},{8,9},{10,11},{12,13},{14,15},{16,17},{18,... | collective-permute-start | bytes 294920 | tf_op jit(solution)/shard_map/ppermute | solution.py:26
  5.3 0.8 copy-start
  6.1 5.3 %copy-start.1 = (bf16[1024,1024]{1,0:T(8,128)(2,1)S(1)}, bf16[1024,1024]{1,0:T(8,128)(2,1)}, u32[]{:S(2)}) copy-start(bf16[1024,1024]{1,0:T(8,128)(2,1)} %constant.11.clone.refs_5_) | copy-start | bytes 6291460
  6.1 5.3 %copy-start.2 = (bf16[512,512]{1,0:T(8,128)(2,1)S(1)}, bf16[512,512]{1,0:T(8,128)(2,1)}, u32[]{:S(2)}) copy-start(bf16[512,512]{1,0:T(8,128)(2,1)} %constant.10.clone.refs_4_) | copy-start | bytes 1572868
  6.1 5.3 %copy-start.3 = (bf16[512,512]{1,0:T(8,128)(2,1)S(1)}, bf16[512,512]{1,0:T(8,128)(2,1)}, u32[]{:S(2)}) copy-start(bf16[512,512]{1,0:T(8,128)(2,1)} %constant.9.clone.refs_3_) | copy-start | bytes 1572868

commit v3 on v2

--- a/solution.py
+++ b/solution.py
@@ -20,18 +20,20 @@
 F32 = jnp.float32
 
 
-def shifted(array, axis, by):
-    count = lax.axis_size(axis)
-    pairs = [(i, i + by) for i in range(count) if 0 <= i + by < count]
-    return lax.ppermute(array, axis, pairs)
+def halo_of(tail):
+    count = lax.axis_size("ta")
+    tail = jnp.where(lax.axis_index("ta") == count - 1, 0, tail).astype(BF16)
+    return lax.ppermute(tail, "ta", [(i, (i + 1) % count) for i in range(count)])
 
 
 def window_rows():
     total_len = TAPS * FRAME
-    positions = np.arange(total_len, dtype=np.float64)
+    tile = lax.broadcasted_iota(jnp.int32, (TAPS * TILES, LANES), 0)
+    lane = lax.broadcasted_iota(jnp.int32, (TAPS * TILES, LANES), 1)
+    positions = (tile * LANES + lane).astype(F32)
     centred = (positions + 0.5 - total_len / 2.0) / FRAME
-    hamming = 0.54 - 0.46 * np.cos(2.0 * np.pi * positions / (total_len - 1))
-    return (np.sinc(centred) * hamming).astype(np.float32).reshape(TAPS * TILES, LANES)
+    hamming = 0.54 - 0.46 * jnp.cos(2.0 * jnp.pi * positions / (total_len - 1))
+    return jnp.sinc(centred) * hamming
 
 
 def dft_rows(first, step, length):
@@ -62,21 +64,18 @@
         f_ref[12 + column, rows, :] = parts[1] - parts[3]
 
 
-def filter_kernel(spec_here, v_hbm, w_hbm, f_ref, head_ref, w_ref, frames, acc, sems, side_sems):
+def filter_kernel(spec_here, v_hbm, w_ref, f_ref, head_ref, frames, acc, sems, head_sem):
     blocks = spec_here // BLOCK
 
     def fetch(b):
         part = pl.ds(b * BLOCK, BLOCK)
         return pltpu.make_async_copy(v_hbm.at[part], frames.at[part], sems.at[b])
 
-    window = pltpu.make_async_copy(w_hbm, w_ref, side_sems.at[0])
-    window.start()
     for b in range(blocks):
         fetch(b).start()
-    head = pltpu.make_async_copy(v_hbm.at[pl.ds(0, BLOCK)], head_ref, side_sems.at[1])
+    head = pltpu.make_async_copy(frames.at[pl.ds(0, BLOCK)], head_ref, head_sem)
+    fetch(0).wait()
     head.start()
-    window.wait()
-    fetch(0).wait()
 
     def step(b, carry):
         fetch(b).wait()
@@ -163,15 +162,14 @@
         out_shape=(
             jax.ShapeDtypeStruct((TILES, 8 * spec_here, LANES), BF16),
             jax.ShapeDtypeStruct((BLOCK, TILES, 8, LANES), jnp.int32),
-            window,
         ),
-        in_specs=[ANY, ANY],
-        out_specs=(VMEM, VMEM, VMEM),
+        in_specs=[ANY, VMEM],
+        out_specs=(VMEM, VMEM),
         scratch_shapes=[
             pltpu.VMEM((spec_here, TILES, 8, LANES), jnp.int32),
             pltpu.VMEM((4, BLOCK * 8, LANES), F32),
             pltpu.SemaphoreType.DMA((spec_here // BLOCK,)),
-            pltpu.SemaphoreType.DMA((2,)),
+            pltpu.SemaphoreType.DMA,
         ],
         compiler_params=pltpu.CompilerParams(vmem_limit_bytes=46 * MIB),
         cost_estimate=pl.CostEstimate(flops=8 * 2 * 1024 * 1024, bytes_accessed=8 * MIB, transcendentals=0),
@@ -215,10 +213,9 @@
     inputs_here, total_len = voltages.shape
     spec_here = total_len // FRAME
     frames = voltages.reshape(inputs_here, spec_here, TILES, LANES).transpose(1, 2, 0, 3)
-    tail = frames[spec_here - (TAPS - 1) :].astype(BF16)
-    halo = shifted(tail, "ta", 1)
-    window = jnp.asarray(window_rows())
-    folded, head, window = filter_call(frames, window)
+    halo = halo_of(frames[spec_here - (TAPS - 1) :])
+    window = window_rows()
+    folded, head = filter_call(frames, window)
     tables = [jnp.asarray(dft_rows(0, 4, 512)), jnp.asarray(dft_rows(2, 4, 512)), jnp.asarray(dft_rows(1, 2, 1024))]
     outgoing = dft_call(head, halo, window, tables, folded)
     arrived = lax.all_to_all(outgoing, ("gx", "ta"), split_axis=0, concat_axis=0, tiled=True)

time: 86.6 us -> 84.1 us (0.971)
  starting transfers between devices: 4.38 us -> 2.55 us
    ppermute x1, starting transfers between devices: 4.38 us -> 2.55 us  [halo_of(): lax.ppermute(tail, 'ta', [(i, (i + 1) % count) for i in range(count)])]
    convert_element_type x0 -> x1, other arithmetic: none -> 0.95 us  [halo_of(): tail = jnp.where(lax.axis_index('ta') == count - 1, 0, tail).astype(BF16)]
    another operation x1 -> x0, other arithmetic: 0.94 us -> none
where the time goes in v3:
time: 84.1 us; the launch traced here: 84 us
  blocking collectives  63.3 us (75%)
  Pallas kernels  16.9 us (20%)
  starting transfers between devices  2.55 us (3%)
  other arithmetic  1.18 us (1%)
    all_to_all x1, blocking collectives, on_device(): lax.all_to_all(outgoing, ('gx', 'ta'), split_axis=0, concat_axis=0, tiled...  63.3 us
    pallas_call x1, Pallas kernels, gram_call(): pl.pallas_call(lambda *refs: gram_kernel(norm, *refs), out_shape=jax.Shap...  6.79 us
    pallas_call x1, Pallas kernels, filter_call(): pl.pallas_call(lambda *refs: filter_kernel(spec_here, *refs), out_shape=(...  5.26 us
    pallas_call x1, Pallas kernels, dft_call(): pl.pallas_call(lambda *refs: dft_kernel(spec_here, *refs), out_shape=(jax...  4.83 us
    ppermute x1, starting transfers between devices, halo_of(): lax.ppermute(tail, 'ta', [(i, (i + 1) % count) for i in range(count)])  2.55 us
  transfers between devices with their start and end apart: 1, of which 0 were waited for; matrix products, arithmetic and copies ran while one was open for 0% of the time, Pallas kernels for 6%

profile of v3, /device:TPU:1, one launch (start us, length us, event | category | flops | bytes accessed | tf_op | source)
XLA Modules:
  0.0 84.0 jit_solution(286431886183309073)
XLA Ops:
  0.0 0.9 %fusion = bf16[3,16,8,128]{3,2,1,0:T(8,128)(2,1)S(1)} fusion(s32[128,16,8,128]{3,2,1,0:T(8,128)} %bitcast.5, pred[]{:T(512)S(6)} %eq.29), kind=kLoop, calls=%fused_computation.1 | loop fusion | flops 98304 | bytes 294913 | tf_op jit(solution)/shard_map/convert_element_type | solution.py:25
  1.0 2.5 %collective-permute-start = (bf16[3,16,8,128]{3,2,1,0:T(8,128)(2,1)S(1)}, bf16[3,16,8,128]{3,2,1,0:T(8,128)(2,1)S(1)}, u32[]{:S(2)}, u32[]{:S(2)}) collective-permute-start(bf16[3,16,8,128]{3,2,1,0:T(8,128)(2,1)S(1)} %fusion), channel_id=1, source_target_pairs={{0,1},{1,0},{2,3},{3,2},{4,5},{5,4},{6,7},{7,6},{8,9},{9,8},{10,11... | collective-permute-start | bytes 294920 | tf_op jit(solution)/shard_map/ppermute | solution.py:26
  3.5 0.2 fusion.5.refs_1_.refs_2_
  3.7 0.0 copy-start
  3.8 0.0 copy-start.1
  3.8 0.0 copy-start.2
  3.8 5.3 %filter.1 = (bf16[16,1024,128]{2,1,0:T(8,128)(2,1)S(1)}, s32[16,16,8,128]{3,2,1,0:T(8,128)S(1)}) custom-call(s32[128,16,8,128]{3,2,1,0:T(8,128)} %bitcast.6, f32[64,128]{1,0:T(8,128)S(1)} %fusion.5.refs_1_.refs_2_), custom_call_target="tpu_custom_call" | custom-call | flops 16777216 | bytes 8388608 | tf_op jit(solution)/shard_map/filter/pallas_call | solution.py:160
  9.0 0.0 collective-permute-done.refs_1_
  9.1 0.0 copy-done
  9.1 0.0 copy-done.1
  9.1 0.0 copy-done.2
  9.1 4.8 %dft.1 = (bf16[128,128,128]{2,1,0:T(8,128)(2,1)S(1)}, bf16[16,1024,128]{2,1,0:T(8,128)(2,1)S(1)}) custom-call(s32[16,16,8,128]{3,2,1,0:T(8,128)S(1)} %get-tuple-element.8.refs_0_, bf16[3,16,8,128]{3,2,1,0:T(8,128)(2,1)S(1)} %collective-permute-done.refs_1_, f32[64,128]{1,0:T(8,128)S(1)} %fusion.5.refs_1_.refs_2_, ...), custom_call_target="tpu_custom_call", output_to_operand_aliasing={{1}: (6, {})} | custom-call | flops 3221225472 | bytes 12582912 | tf_op jit(solution)/shard_map/dft/pallas_call | solution.py:182
  13.9 63.3 %all_to_all.5 = bf16[128,128,128]{2,1,0:T(8,128)(2,1)S(1)} all-to-all(bf16[128,128,128]{2,1,0:T(8,128)(2,1)S(1)} %get-tuple-element.10), channel_id=1, replica_groups=mesh['gx'=64,'ta'=2] {'gx','ta'}, dimensions={0} | all-to-all | bytes 8388608 | tf_op jit(solution)/shard_map/all_to_all | solution.py:221
  77.2 6.8 %gram.1 = f32[8,2,512,512]{3,2,1,0:T(8,128)} custom-call(bf16[64,2,128,128]{3,2,1,0:T(8,128)(2,1)S(1)} %bitcast.4), custom_call_target="tpu_custom_call" | custom-call | flops 4294967296 | bytes 20971520 | tf_op jit(solution)/shard_map/gram/pallas_call | solution.py:196
  (1 shorter events, 0.0 us)
Async XLA Ops:
  1.0 8.1 %collective-permute-start = (bf16[3,16,8,128]{3,2,1,0:T(8,128)(2,1)S(1)}, bf16[3,16,8,128]{3,2,1,0:T(8,128)(2,1)S(1)}, u32[]{:S(2)}, u32[]{:S(2)}) collective-permute-start(bf16[3,16,8,128]{3,2,1,0:T(8,128)(2,1)S(1)} %fusion), channel_id=1, source_target_pairs={{0,1},{1,0},{2,3},{3,2},{4,5},{5,4},{6,7},{7,6},{8,9},{9,8},{10,11... | collective-permute-start | bytes 294920 | tf_op jit(solution)/shard_map/ppermute | solution.py:26
  3.7 5.3 %copy-start = (bf16[1024,1024]{1,0:T(8,128)(2,1)S(1)}, bf16[1024,1024]{1,0:T(8,128)(2,1)}, u32[]{:S(2)}) copy-start(bf16[1024,1024]{1,0:T(8,128)(2,1)} %constant.74.clone.refs_5_) | copy-start | bytes 6291460
  3.8 5.3 %copy-start.1 = (bf16[512,512]{1,0:T(8,128)(2,1)S(1)}, bf16[512,512]{1,0:T(8,128)(2,1)}, u32[]{:S(2)}) copy-start(bf16[512,512]{1,0:T(8,128)(2,1)} %constant.73.clone.refs_4_) | copy-start | bytes 1572868
  3.8 5.3 %copy-start.2 = (bf16[512,512]{1,0:T(8,128)(2,1)S(1)}, bf16[512,512]{1,0:T(8,128)(2,1)}, u32[]{:S(2)}) copy-start(bf16[512,512]{1,0:T(8,128)(2,1)} %constant.72.clone.refs_3_) | copy-start | bytes 1572868

commit v4 on v3

--- a/solution.py
+++ b/solution.py
@@ -44,16 +44,18 @@
     return rows.reshape(2 * chan.size, length).astype(BF16)
 
 
-def filter_block(frame_at, w_ref, acc_ref, f_ref, column, block, spec_here):
-    for q in range(4):
-        tile = column + 4 * q
-        weights = [jnp.broadcast_to(w_ref[pl.ds(t * TILES + tile, 1), :], (8, LANES)) for t in range(TAPS)]
-        frames = [frame_at(f, tile).astype(F32) for f in range(BLOCK + TAPS - 1)]
-        for s in range(BLOCK):
-            total = weights[0] * frames[s] + weights[1] * frames[s + 1]
-            total = total + weights[2] * frames[s + 2] + weights[3] * frames[s + 3]
-            acc_ref[q, s * 8 : (s + 1) * 8, :] = total
-    for i in range(8):
+def filter_taps(frame_at, w_ref, acc_ref, column, q):
+    tile = column + 4 * q
+    weights = [jnp.broadcast_to(w_ref[pl.ds(t * TILES + tile, 1), :], (8, LANES)) for t in range(TAPS)]
+    frames = [frame_at(f, tile).astype(F32) for f in range(BLOCK + TAPS - 1)]
+    for s in range(BLOCK):
+        total = weights[0] * frames[s] + weights[1] * frames[s + 1]
+        total = total + weights[2] * frames[s + 2] + weights[3] * frames[s + 3]
+        acc_ref[q, s * 8 : (s + 1) * 8, :] = total
+
+
+def filter_fold(acc_ref, f_ref, column, block, spec_here, inputs):
+    for i in inputs:
         parts = [acc_ref[q, pl.ds(i, BLOCK, stride=8), :].astype(BF16) for q in range(4)]
         wide = [part.astype(F32) for part in parts]
         evens, odds = wide[0] + wide[2], wide[1] + wide[3]
@@ -64,35 +66,47 @@
         f_ref[12 + column, rows, :] = parts[1] - parts[3]
 
 
-def filter_kernel(spec_here, v_hbm, w_ref, f_ref, head_ref, frames, acc, sems, head_sem):
+def filter_block(frame_at, w_ref, acc_ref, f_ref, column, block, spec_here):
+    for q in range(4):
+        filter_taps(frame_at, w_ref, acc_ref, column, q)
+    filter_fold(acc_ref, f_ref, column, block, spec_here, range(8))
+
+
+def filter_kernel(spec_here, v_hbm, w_ref, f_ref, head_ref, frames, acc_even, acc_odd, sems, head_sem):
     blocks = spec_here // BLOCK
+    accs = (acc_even, acc_odd)
 
     def fetch(b):
         part = pl.ds(b * BLOCK, BLOCK)
         return pltpu.make_async_copy(v_hbm.at[part], frames.at[part], sems.at[b])
 
-    for b in range(blocks):
+    first = pltpu.make_async_copy(v_hbm.at[pl.ds(BLOCK - 3, 3)], frames.at[pl.ds(BLOCK - 3, 3)], sems.at[0])
+    first.start()
+    for b in range(1, blocks):
         fetch(b).start()
-    head = pltpu.make_async_copy(frames.at[pl.ds(0, BLOCK)], head_ref, head_sem)
-    fetch(0).wait()
+    head = pltpu.make_async_copy(v_hbm.at[pl.ds(0, BLOCK)], head_ref, head_sem)
     head.start()
+    first.wait()
 
     def step(b, carry):
         fetch(b).wait()
 
-        def columns(column, carry):
-            filter_block(
-                lambda f, tile: frames[b * BLOCK - (TAPS - 1) + f, tile], w_ref, acc, f_ref, column, b, spec_here
-            )
-            return carry
-
-        return lax.fori_loop(0, 4, columns, carry)
+        def frame_at(f, tile):
+            return frames[b * BLOCK - (TAPS - 1) + f, tile]
+
+        for column in range(5):
+            for q in range(4):
+                if column < 4:
+                    filter_taps(frame_at, w_ref, accs[column % 2], column, q)
+                if column > 0:
+                    filter_fold(accs[(column - 1) % 2], f_ref, column - 1, b, spec_here, range(2 * q, 2 * q + 2))
+        return carry
 
     lax.fori_loop(1, blocks, step, 0)
     head.wait()
 
 
-def dft_kernel(spec_here, head_ref, halo_ref, w_ref, t0_ref, t1_ref, t2_ref, f_in, out_ref, f_ref, acc, scr):
+def dft_kernel(spec_here, head_ref, halo_ref, w_ref, t0_ref, t1_ref, t2_ref, f_in, out_ref, f_ref, acc, *results):
     def first(column, carry):
         def frame_at(f, tile):
             return halo_ref[f, tile] if f < TAPS - 1 else head_ref[f - (TAPS - 1), tile]
@@ -103,22 +117,38 @@
     lax.fori_loop(0, 4, first, 0)
     scale = 1.0 / (64.0 * math.sqrt(FRAME))
     pair = 2 * spec_here
-    groups = ((t0_ref, 0, 0, 0, 32), (t1_ref, 4, 4096, 32, 32), (t2_ref, 8, 8192, 64, 64))
-    for table, column, base, place, each in groups:
-        rows_all, length = table.shape
-        for ip in range(4):
-            right = jnp.concatenate(
-                [f_ref[column + c, ip * pair : (ip + 1) * pair, :] for c in range(length // LANES)], axis=1
-            )
-            for part in range(rows_all // 512):
-                left = table[part * 512 : (part + 1) * 512, :]
-                sums = lax.dot_general(left, right, (((1,), (1,)), ((), ())), preferred_element_type=F32) * scale
-                for side in range(2):
-                    rows = pl.ds(base + part * 4096 + ip * 2 + side, 512, stride=8)
-                    scr[rows, :] = sums[:, side * spec_here : (side + 1) * spec_here]
-        for d in range(0, 128, 4):
-            rows = scr[base + d * each : base + (d + 4) * each, :].astype(BF16)
-            out_ref[d : d + 4, place : place + each, :] = rows.reshape(4, each, LANES)
+    tasks = [
+        (t2_ref, 0, 8, results[0], 64, 64, 0),
+        (t2_ref, 512, 8, results[1], 64, 64, 64),
+        (t0_ref, 0, 0, results[2], 0, 32, 0),
+        (t1_ref, 0, 4, results[3], 32, 32, 0),
+    ]
+
+    def multiply(task, ip):
+        table, first_row, column, result = task[:4]
+        length = table.shape[1]
+        right = jnp.concatenate(
+            [f_ref[column + c, ip * pair : (ip + 1) * pair, :] for c in range(length // LANES)], axis=1
+        )
+        left = table[first_row : first_row + 512, :]
+        sums = lax.dot_general(left, right, (((1,), (1,)), ((), ())), preferred_element_type=F32) * scale
+        for side in range(2):
+            result[pl.ds(ip * 2 + side, 512, stride=9), :] = sums[:, side * spec_here : (side + 1) * spec_here]
+
+    def emit(task, quarter):
+        result, place, each, start = task[3:]
+        count = 4096 // each // 4
+        for d in range(quarter * count, (quarter + 1) * count, 4):
+            rows = [result[r * 9 : r * 9 + 8, :] for r in range(d * each // 8, (d + 4) * each // 8)]
+            rows = jnp.concatenate(rows, axis=0).astype(BF16)
+            out_ref[start + d : start + d + 4, place : place + each, :] = rows.reshape(4, each, LANES)
+
+    for n in range(len(tasks) + 1):
+        for quarter in range(4):
+            if n < len(tasks):
+                multiply(tasks[n], quarter)
+            if n > 0:
+                emit(tasks[n - 1], quarter)
 
 
 def gram_kernel(norm, got_ref, out_hbm, mats, out, sems):
@@ -168,6 +198,7 @@
         scratch_shapes=[
             pltpu.VMEM((spec_here, TILES, 8, LANES), jnp.int32),
             pltpu.VMEM((4, BLOCK * 8, LANES), F32),
+            pltpu.VMEM((4, BLOCK * 8, LANES), F32),
             pltpu.SemaphoreType.DMA((spec_here // BLOCK,)),
             pltpu.SemaphoreType.DMA,
         ],
@@ -185,7 +216,7 @@
         in_specs=[VMEM] * 7,
         out_specs=(VMEM, VMEM),
         input_output_aliases={6: 1},
-        scratch_shapes=[pltpu.VMEM((4, BLOCK * 8, LANES), F32), pltpu.VMEM((8 * FRAME, spec_here), F32)],
+        scratch_shapes=[pltpu.VMEM((4, BLOCK * 8, LANES), F32)] + [pltpu.VMEM((9 * 512, spec_here), F32)] * 4,
         compiler_params=pltpu.CompilerParams(vmem_limit_bytes=40 * MIB),
         cost_estimate=pl.CostEstimate(flops=3 * 1024**3, bytes_accessed=12 * MIB, transcendentals=0),
         name="dft",

time: 84.1 us -> 83.1 us (0.988)
  Pallas kernels: 16.9 us -> 15.9 us
where the time goes in v4:
time: 83.1 us; the launch traced here: 83 us
  blocking collectives  63.3 us (76%)
  Pallas kernels  15.9 us (19%)
  starting transfers between devices  2.55 us (3%)
  other arithmetic  1.18 us (1%)
    all_to_all x1, blocking collectives, on_device(): lax.all_to_all(outgoing, ('gx', 'ta'), split_axis=0, concat_axis=0, tiled...  63.3 us
    pallas_call x1, Pallas kernels, gram_call(): pl.pallas_call(lambda *refs: gram_kernel(norm, *refs), out_shape=jax.Shap...  6.79 us
    pallas_call x1, Pallas kernels, filter_call(): pl.pallas_call(lambda *refs: filter_kernel(spec_here, *refs), out_shape=(...  4.79 us
    pallas_call x1, Pallas kernels, dft_call(): pl.pallas_call(lambda *refs: dft_kernel(spec_here, *refs), out_shape=(jax...  4.28 us
    ppermute x1, starting transfers between devices, halo_of(): lax.ppermute(tail, 'ta', [(i, (i + 1) % count) for i in range(count)])  2.55 us
  transfers between devices with their start and end apart: 1, of which 0 were waited for; matrix products, arithmetic and copies ran while one was open for 0% of the time, Pallas kernels for 6%

profile of v4, /device:TPU:1, one launch (start us, length us, event | category | flops | bytes accessed | tf_op | source)
XLA Modules:
  0.0 83.0 jit_solution(1996297704107696565)
XLA Ops:
  0.0 0.9 %fusion = bf16[3,16,8,128]{3,2,1,0:T(8,128)(2,1)S(1)} fusion(s32[128,16,8,128]{3,2,1,0:T(8,128)} %bitcast.5, pred[]{:T(512)S(6)} %eq.29), kind=kLoop, calls=%fused_computation.1 | loop fusion | flops 98304 | bytes 294913 | tf_op jit(solution)/shard_map/convert_element_type | solution.py:25
  1.0 2.5 %collective-permute-start = (bf16[3,16,8,128]{3,2,1,0:T(8,128)(2,1)S(1)}, bf16[3,16,8,128]{3,2,1,0:T(8,128)(2,1)S(1)}, u32[]{:S(2)}, u32[]{:S(2)}) collective-permute-start(bf16[3,16,8,128]{3,2,1,0:T(8,128)(2,1)S(1)} %fusion), channel_id=1, source_target_pairs={{0,1},{1,0},{2,3},{3,2},{4,5},{5,4},{6,7},{7,6},{8,9},{9,8},{10,11... | collective-permute-start | bytes 294920 | tf_op jit(solution)/shard_map/ppermute | solution.py:26
  3.5 0.2 fusion.5.refs_1_.refs_2_
  3.7 0.0 copy-start
  3.8 0.0 copy-start.1
  3.8 0.0 copy-start.2
  3.8 4.8 %filter.1 = (bf16[16,1024,128]{2,1,0:T(8,128)(2,1)S(1)}, s32[16,16,8,128]{3,2,1,0:T(8,128)S(1)}) custom-call(s32[128,16,8,128]{3,2,1,0:T(8,128)} %bitcast.6, f32[64,128]{1,0:T(8,128)S(1)} %fusion.5.refs_1_.refs_2_), custom_call_target="tpu_custom_call" | custom-call | flops 16777216 | bytes 8388608 | tf_op jit(solution)/shard_map/filter/pallas_call | solution.py:190
  8.6 0.0 collective-permute-done.refs_1_
  8.6 0.0 copy-done
  8.6 0.0 copy-done.1
  8.6 0.0 copy-done.2
  8.6 4.3 %dft.1 = (bf16[128,128,128]{2,1,0:T(8,128)(2,1)S(1)}, bf16[16,1024,128]{2,1,0:T(8,128)(2,1)S(1)}) custom-call(s32[16,16,8,128]{3,2,1,0:T(8,128)S(1)} %get-tuple-element.8.refs_0_, bf16[3,16,8,128]{3,2,1,0:T(8,128)(2,1)S(1)} %collective-permute-done.refs_1_, f32[64,128]{1,0:T(8,128)S(1)} %fusion.5.refs_1_.refs_2_, ...), custom_call_target="tpu_custom_call", output_to_operand_aliasing={{1}: (6, {})} | custom-call | flops 3221225472 | bytes 12582912 | tf_op jit(solution)/shard_map/dft/pallas_call | solution.py:213
  12.9 63.3 %all_to_all.5 = bf16[128,128,128]{2,1,0:T(8,128)(2,1)S(1)} all-to-all(bf16[128,128,128]{2,1,0:T(8,128)(2,1)S(1)} %get-tuple-element.10), channel_id=1, replica_groups=mesh['gx'=64,'ta'=2] {'gx','ta'}, dimensions={0} | all-to-all | bytes 8388608 | tf_op jit(solution)/shard_map/all_to_all | solution.py:252
  76.2 6.8 %gram.1 = f32[8,2,512,512]{3,2,1,0:T(8,128)} custom-call(bf16[64,2,128,128]{3,2,1,0:T(8,128)(2,1)S(1)} %bitcast.4), custom_call_target="tpu_custom_call" | custom-call | flops 4294967296 | bytes 20971520 | tf_op jit(solution)/shard_map/gram/pallas_call | solution.py:227
  (1 shorter events, 0.0 us)
Async XLA Ops:
  1.0 7.6 %collective-permute-start = (bf16[3,16,8,128]{3,2,1,0:T(8,128)(2,1)S(1)}, bf16[3,16,8,128]{3,2,1,0:T(8,128)(2,1)S(1)}, u32[]{:S(2)}, u32[]{:S(2)}) collective-permute-start(bf16[3,16,8,128]{3,2,1,0:T(8,128)(2,1)S(1)} %fusion), channel_id=1, source_target_pairs={{0,1},{1,0},{2,3},{3,2},{4,5},{5,4},{6,7},{7,6},{8,9},{9,8},{10,11... | collective-permute-start | bytes 294920 | tf_op jit(solution)/shard_map/ppermute | solution.py:26
  3.7 4.8 %copy-start = (bf16[1024,1024]{1,0:T(8,128)(2,1)S(1)}, bf16[1024,1024]{1,0:T(8,128)(2,1)}, u32[]{:S(2)}) copy-start(bf16[1024,1024]{1,0:T(8,128)(2,1)} %constant.74.clone.refs_5_) | copy-start | bytes 6291460
  3.8 4.8 %copy-start.1 = (bf16[512,512]{1,0:T(8,128)(2,1)S(1)}, bf16[512,512]{1,0:T(8,128)(2,1)}, u32[]{:S(2)}) copy-start(bf16[512,512]{1,0:T(8,128)(2,1)} %constant.73.clone.refs_4_) | copy-start | bytes 1572868
  3.8 4.8 %copy-start.2 = (bf16[512,512]{1,0:T(8,128)(2,1)S(1)}, bf16[512,512]{1,0:T(8,128)(2,1)}, u32[]{:S(2)}) copy-start(bf16[512,512]{1,0:T(8,128)(2,1)} %constant.72.clone.refs_3_) | copy-start | bytes 1572868

commit v5 on v3

v5 whole, which is shorter than its diff:
```python
import functools
import math

import jax
import jax.numpy as jnp
import numpy as np
from jax import lax
from jax.experimental import pallas as pl
from jax.experimental.pallas import tpu as pltpu
from jax.sharding import PartitionSpec as P

INPUTS = 512
CHAN = 1024
TAPS = 4
FRAME = 2 * CHAN
LANES = 128
TILES = FRAME // LANES
BLOCK = 16
HALF = 64
MIB = 1024 * 1024
BF16 = jnp.bfloat16
F32 = jnp.float32


def halo_of(tail):
    count = lax.axis_size("ta")
    return lax.ppermute(tail, "ta", [(i, (i + 1) % count) for i in range(count)])


def window_rows():
    total_len = TAPS * FRAME
    tile = lax.broadcasted_iota(jnp.int32, (TAPS * TILES, LANES), 0)
    lane = lax.broadcasted_iota(jnp.int32, (TAPS * TILES, LANES), 1)
    positions = (tile * LANES + lane).astype(F32)
    centred = (positions + 0.5 - total_len / 2.0) / FRAME
    hamming = 0.54 - 0.46 * jnp.cos(2.0 * jnp.pi * positions / (total_len - 1))
    return jnp.sinc(centred) * hamming


def dft_rows(first, step, length):
    chan = np.arange(first, CHAN, step)
    phase = chan[:, None] * np.arange(length)[None, :] % FRAME
    angle = phase * (2.0 * np.pi / FRAME)
    rows = np.stack([np.cos(angle), -np.sin(angle)], axis=1)
    return rows.reshape(2 * chan.size, length).astype(BF16)


def filter_taps(frame_at, w_ref, acc_ref, column, q):
    tile = column + 4 * q
    weights = [jnp.broadcast_to(w_ref[pl.ds(t * TILES + tile, 1), :], (8, LANES)) for t in range(TAPS)]
    frames = [frame_at(f, tile).astype(F32) for f in range(BLOCK + TAPS - 1)]
    for s in range(BLOCK):
        total = weights[0] * frames[s] + weights[1] * frames[s + 1]
        total = total + weights[2] * frames[s + 2] + weights[3] * frames[s + 3]
        acc_ref[q, s * 8 : (s + 1) * 8, :] = total


def filter_fold(acc_ref, f_ref, column, block, inputs):
    for i in inputs:
        parts = [acc_ref[q, pl.ds(i, BLOCK, stride=8), :].astype(BF16) for q in range(4)]
        wide = [part.astype(F32) for part in parts]
        evens, odds = wide[0] + wide[2], wide[1] + wide[3]
        rows = pl.ds(pl.multiple_of((i % 4) * LANES + (i // 4) * HALF + block * BLOCK, BLOCK), BLOCK)
        f_ref[column, rows, :] = (evens + odds).astype(BF16)
        f_ref[4 + column, rows, :] = (evens - odds).astype(BF16)
        f_ref[8 + column, rows, :] = parts[0] - parts[2]
        f_ref[12 + column, rows, :] = parts[1] - parts[3]


def filter_block(frame_at, w_ref, accs, f_ref, block):
    for column in range(5):
        for q in range(4):
            if column < 4:
                filter_taps(frame_at, w_ref, accs[column % 2], column, q)
            if column > 0:
                filter_fold(accs[(column - 1) % 2], f_ref, column - 1, block, range(2 * q, 2 * q + 2))


def transform(f_ref, tables, results, out_ref, half):
    t0_ref, t1_ref, t2_ref = tables
    scale = 1.0 / (64.0 * math.sqrt(FRAME))
    tasks = [
        (t2_ref, 0, 8, results[0], 32, 32, 0),
        (t2_ref, 512, 8, results[1], 32, 32, 64),
        (t0_ref, 0, 0, results[2], 0, 16, 0),
        (t1_ref, 0, 4, results[3], 16, 16, 0),
    ]

    def multiply(task, pair):
        table, first_row, column, result = task[:4]
        right = [f_ref[column + c, pair * 256 : (pair + 1) * 256, :] for c in range(table.shape[1] // LANES)]
        left = table[first_row : first_row + 512, :]
        dims = (((1,), (1,)), ((), ()))
        sums = lax.dot_general(left, jnp.concatenate(right, axis=1), dims, preferred_element_type=F32) * scale
        for side in range(2):
            result[pl.ds(pair * 2 + side, 512, stride=4), :] = sums[:, side * LANES : (side + 1) * LANES]

    def emit(task, part):
        result, place, each, start = task[3:]
        place = place + half * 64
        count = 2048 // each // 2
        for d in range(part * count, (part + 1) * count, 4):
            rows = result[d * each : (d + 4) * each, :].astype(BF16)
            out_ref[start + d : start + d + 4, place : place + each, :] = rows.reshape(4, each, LANES)

    for n in range(len(tasks) + 1):
        for part in range(2):
            if n < len(tasks):
                multiply(tasks[n], part)
            if n > 0:
                emit(tasks[n - 1], part)


def late_kernel(spec_here, v_hbm, w_ref, f_ref, tail_ref, frames, acc_even, acc_odd, sems):
    begin = spec_here // 2 - (TAPS - 1)
    blocks = HALF // BLOCK

    def fetch(first, count, sem):
        rows = pl.ds(first, count)
        return pltpu.make_async_copy(v_hbm.at[pl.ds(begin + first, count)], frames.at[rows], sems.at[sem])

    fetch(0, TAPS - 1, blocks).start()
    for b in range(blocks):
        fetch(TAPS - 1 + b * BLOCK, BLOCK, b).start()
    fetch(0, TAPS - 1, blocks).wait()

    def step(b, carry):
        fetch(TAPS - 1 + b * BLOCK, BLOCK, b).wait()
        filter_block(lambda f, tile: frames[b * BLOCK + f, tile], w_ref, (acc_even, acc_odd), f_ref, b)
        return carry

    lax.fori_loop(0, blocks, step, 0)
    keep = jnp.where(lax.axis_index("ta") == lax.axis_size("ta") - 1, 0.0, 1.0).astype(F32)
    for f in range(TAPS - 1):
        tail_ref[f] = (frames[HALF + f].astype(F32) * keep).astype(BF16)


def middle_kernel(v_hbm, w_ref, late_ref, t0_ref, t1_ref, t2_ref, out_ref, f_ref, head_ref, frames, acc_even, acc_odd, sems, *results):
    begin = BLOCK - (TAPS - 1)
    blocks = HALF // BLOCK

    def fetch(first, count, sem):
        rows = pl.ds(first, count)
        return pltpu.make_async_copy(v_hbm.at[pl.ds(begin + first, count)], frames.at[rows], sems.at[sem])

    fetch(0, TAPS - 1, 0).start()
    for b in range(1, blocks):
        fetch(TAPS - 1 + (b - 1) * BLOCK, BLOCK, b).start()
    head = pltpu.make_async_copy(v_hbm.at[pl.ds(0, BLOCK)], head_ref, sems.at[blocks])
    head.start()
    transform(late_ref, (t0_ref, t1_ref, t2_ref), results, out_ref, 1)
    fetch(0, TAPS - 1, 0).wait()

    def step(b, carry):
        fetch(TAPS - 1 + (b - 1) * BLOCK, BLOCK, b).wait()
        filter_block(lambda f, tile: frames[(b - 1) * BLOCK + f, tile], w_ref, (acc_even, acc_odd), f_ref, b)
        return carry

    lax.fori_loop(1, blocks, step, 0)
    head.wait()


def early_kernel(head_ref, halo_ref, w_ref, t0_ref, t1_ref, t2_ref, f_in, out_in, out_ref, f_ref, acc_even, acc_odd, *results):
    def frame_at(f, tile):
        return halo_ref[f, tile] if f < TAPS - 1 else head_ref[f - (TAPS - 1), tile]

    filter_block(frame_at, w_ref, (acc_even, acc_odd), f_ref, 0)
    transform(f_ref, (t0_ref, t1_ref, t2_ref), results, out_ref, 0)


def gram_kernel(norm, got_ref, out_hbm, mats, out, sems):
    def copy_out(k, p):
        return pltpu.make_async_copy(out.at[k, p], out_hbm.at[k, p], sems.at[k, p])

    low = lax.broadcasted_iota(jnp.int32, (64, 8, LANES), 2) < HALF
    upper = lax.broadcasted_iota(jnp.int32, (64, 8, LANES), 1) < 4

    def sort(first, second):
        one = jnp.where(low, first, pltpu.roll(second, HALF, 2))
        two = jnp.where(low, pltpu.roll(first, HALF, 2), second)
        real = jnp.where(upper, one, pltpu.roll(two, 4, 1))
        imag = jnp.where(upper, pltpu.roll(one, 4, 1), two)
        return real.reshape(INPUTS, LANES).astype(BF16), imag.reshape(INPUTS, LANES).astype(BF16)

    for group, channels in enumerate(((0, 4), (2, 6), (1, 3), (5, 7))):
        for ta in range(2):
            halves = [got_ref[:, ta, h * 64 + group * 16 : h * 64 + (group + 1) * 16, :].astype(F32) for h in range(2)]
            for u in range(2):
                mat = mats.at[u]
                real, imag = sort(*[x[:, u * 8 : (u + 1) * 8, :] for x in halves])
                mat[:INPUTS, ta * 128 : (ta + 1) * 128] = real
                mat[:INPUTS, 256 + ta * 128 : 256 + (ta + 1) * 128] = imag
                mat[INPUTS:, ta * 128 : (ta + 1) * 128] = imag
                mat[INPUTS:, 256 + ta * 128 : 256 + (ta + 1) * 128] = -real
        for u, k in enumerate(channels):
            for p in range(2):
                left = mats[u, p * INPUTS : (p + 1) * INPUTS, :]
                dims = (((1,), (1,)), ((), ()))
                gram = lax.dot_general(left, mats[u, :INPUTS, :], dims, preferred_element_type=F32)
                out[k, p] = gram * norm
                copy_out(k, p).start()
    for k in range(8):
        for p in range(2):
            copy_out(k, p).wait()


VMEM = pl.BlockSpec(memory_space=pltpu.VMEM)
ANY = pl.BlockSpec(memory_space=pl.ANY)
FOLDED = jax.ShapeDtypeStruct((TILES, 8 * HALF, LANES), BF16)
PAYLOAD = jax.ShapeDtypeStruct((128, 128, LANES), BF16)
ACCS = [pltpu.VMEM((4, BLOCK * 8, LANES), F32)] * 2
RESULTS = [pltpu.VMEM((512 * 4, LANES), F32)] * 4


def late_call(frames, window):
    return pl.pallas_call(
        functools.partial(late_kernel, frames.shape[0]),
        out_shape=(FOLDED, jax.ShapeDtypeStruct((TAPS - 1, TILES, 8, LANES), BF16)),
        in_specs=[ANY, VMEM],
        out_specs=(VMEM, VMEM),
        scratch_shapes=[pltpu.VMEM((HALF + TAPS - 1, TILES, 8, LANES), jnp.int32)]
        + ACCS
        + [pltpu.SemaphoreType.DMA((HALF // BLOCK + 1,))],
        compiler_params=pltpu.CompilerParams(vmem_limit_bytes=46 * MIB),
        cost_estimate=pl.CostEstimate(flops=8 * 1024 * 1024, bytes_accessed=4 * MIB, transcendentals=0),
        name="late",
    )(frames, window)


def middle_call(frames, window, late, tables):
    return pl.pallas_call(
        middle_kernel,
        out_shape=(PAYLOAD, FOLDED, jax.ShapeDtypeStruct((BLOCK, TILES, 8, LANES), jnp.int32)),
        in_specs=[ANY] + [VMEM] * 5,
        out_specs=(VMEM, VMEM, VMEM),
        scratch_shapes=[pltpu.VMEM((HALF - BLOCK + TAPS - 1, TILES, 8, LANES), jnp.int32)]
        + ACCS
        + [pltpu.SemaphoreType.DMA((HALF // BLOCK + 1,))]
        + RESULTS,
        compiler_params=pltpu.CompilerParams(vmem_limit_bytes=40 * MIB),
        cost_estimate=pl.CostEstimate(flops=2 * 1024**3, bytes_accessed=12 * MIB, transcendentals=0),
        name="middle",
    )(frames, window, late, *tables)


def early_call(head, halo, window, tables, folded, payload):
    return pl.pallas_call(
        early_kernel,
        out_shape=(PAYLOAD, FOLDED),
        in_specs=[VMEM] * 8,
        out_specs=(VMEM, VMEM),
        input_output_aliases={6: 1, 7: 0},
        scratch_shapes=ACCS + RESULTS,
        compiler_params=pltpu.CompilerParams(vmem_limit_bytes=40 * MIB),
        cost_estimate=pl.CostEstimate(flops=2 * 1024**3, bytes_accessed=8 * MIB, transcendentals=0),
        name="early",
    )(head, halo, window, *tables, folded, payload)[0]


def gram_call(arrived, norm):
    return pl.pallas_call(
        lambda *refs: gram_kernel(norm, *refs),
        out_shape=jax.ShapeDtypeStruct((8, 2, INPUTS, INPUTS), F32),
        in_specs=[VMEM],
        out_specs=ANY,
        scratch_shapes=[
            pltpu.VMEM((2, 2 * INPUTS, 512), BF16),
            pltpu.VMEM((8, 2, INPUTS, INPUTS), F32),
            pltpu.SemaphoreType.DMA((8, 2)),
        ],
        compiler_params=pltpu.CompilerParams(vmem_limit_bytes=40 * MIB),
        cost_estimate=pl.CostEstimate(flops=4 * 1024**3, bytes_accessed=20 * MIB, transcendentals=0),
        name="gram",
    )(arrived)


def on_device(voltages):
    inputs_here, total_len = voltages.shape
    spec_here = total_len // FRAME
    frames = voltages.reshape(inputs_here, spec_here, TILES, LANES).transpose(1, 2, 0, 3)
    window = window_rows()
    tables = [jnp.asarray(dft_rows(0, 4, 512)), jnp.asarray(dft_rows(2, 4, 512)), jnp.asarray(dft_rows(1, 2, 1024))]
    late, tail = late_call(frames, window)
    halo = halo_of(tail)
    payload, folded, head = middle_call(frames, window, late, tables)
    outgoing = early_call(head, halo, window, tables, folded, payload)
    arrived = lax.all_to_all(outgoing, ("gx", "ta"), split_axis=0, concat_axis=0, tiled=True)
    norm = 1.0 / math.sqrt(2 * spec_here)
    return gram_call(arrived.reshape(64, 2, 128, spec_here), norm)


def solution(mesh):
    placed = (P("gx", "ta"),)
    return jax.shard_map(
        on_device,
        mesh=mesh,
        in_specs=placed,
        out_specs=P(("gx", "ta"), None, None, None),
        check_vma=False,
    )
```

time: 84.1 us -> 82.5 us (0.981)
  other arithmetic: 1.18 us -> 0.24 us
    convert_element_type x1 -> x0, other arithmetic: 0.95 us -> none  [halo_of(): tail = jnp.where(lax.axis_index('ta') == count - 1, 0, tail).astype(BF16)]
    pallas_call x2 -> x3, Pallas kernels: 10.1 us -> 9.42 us  [the longest x1 3.72 us: middle_call(): pl.pallas_call(middle_kernel, out_shape=(PAYLOAD, FOLDED, jax.ShapeDtypeS...]
  transfers between devices with their start and end apart: 1 -> 1, of which waited for: 0 -> 0; matrix products, arithmetic and copies ran while one was open for 0% -> 0% of each run, Pallas kernels for 6% -> 5%
where the time goes in v5:
time: 82.5 us; the launch traced here: 82.4 us
  blocking collectives  63.3 us (77%)
  Pallas kernels  16.3 us (20%)
  starting transfers between devices  2.55 us (3%)
    all_to_all x1, blocking collectives, on_device(): lax.all_to_all(outgoing, ('gx', 'ta'), split_axis=0, concat_axis=0, tiled...  63.3 us
    pallas_call x1, Pallas kernels, gram_call(): pl.pallas_call(lambda *refs: gram_kernel(norm, *refs), out_shape=jax.Shap...  6.84 us
    pallas_call x1, Pallas kernels, middle_call(): pl.pallas_call(middle_kernel, out_shape=(PAYLOAD, FOLDED, jax.ShapeDtypeS...  3.72 us
    pallas_call x1, Pallas kernels, late_call(): pl.pallas_call(functools.partial(late_kernel, frames.shape[0]), out_shape...  3.38 us
    ppermute x1, starting transfers between devices, halo_of(): lax.ppermute(tail, 'ta', [(i, (i + 1) % count) for i in range(count)])  2.55 us
    pallas_call x1, Pallas kernels, early_call(): pl.pallas_call(early_kernel, out_shape=(PAYLOAD, FOLDED), in_specs=[VMEM]...  2.32 us
  transfers between devices with their start and end apart: 1, of which 0 were waited for; matrix products, arithmetic and copies ran while one was open for 0% of the time, Pallas kernels for 5%

profile of v5, /device:TPU:1, one launch (start us, length us, event | category | flops | bytes accessed | tf_op | source)
XLA Modules:
  0.0 82.4 jit_solution(14509831916995022663)
XLA Ops:
  0.0 0.2 fusion.4.w_ref
  0.2 0.0 copy-start
  0.3 0.0 copy-start.1
  0.3 0.0 copy-start.2
  0.3 3.4 %late.1 = (bf16[16,512,128]{2,1,0:T(8,128)(2,1)S(1)}, bf16[3,16,8,128]{3,2,1,0:T(8,128)(2,1)S(1)}) custom-call(s32[128,16,8,128]{3,2,1,0:T(8,128)} %bitcast.5, f32[64,128]{1,0:T(8,128)S(1)} %fusion.4.w_ref), custom_call_target="tpu_custom_call" | custom-call | flops 8388608 | bytes 4194304 | tf_op jit(solution)/shard_map/late/pallas_call | solution.py:216
  3.7 2.5 %collective-permute-start = (bf16[3,16,8,128]{3,2,1,0:T(8,128)(2,1)S(1)}, bf16[3,16,8,128]{3,2,1,0:T(8,128)(2,1)S(1)}, u32[]{:S(2)}, u32[]{:S(2)}) collective-permute-start(bf16[3,16,8,128]{3,2,1,0:T(8,128)(2,1)S(1)} %get-tuple-element.13), channel_id=1, source_target_pairs={{0,1},{1,0},{2,3},{3,2},{4,5},{5,4},{6,7},{7,6},{8,9},{9,8},{10,11... | collective-permute-start | bytes 294920 | tf_op jit(solution)/shard_map/ppermute | solution.py:27
  6.2 0.0 copy-done
  6.2 0.0 copy-done.1
  6.2 0.0 copy-done.2
  6.2 3.7 %middle.1 = (bf16[128,128,128]{2,1,0:T(8,128)(2,1)S(1)}, bf16[16,512,128]{2,1,0:T(8,128)(2,1)S(1)}, s32[16,16,8,128]{3,2,1,0:T(8,128)S(1)}) custom-call(s32[128,16,8,128]{3,2,1,0:T(8,128)} %bitcast.6, f32[64,128]{1,0:T(8,128)S(1)} %fusion.4.w_ref, bf16[16,512,128]{2,1,0:T(8,128)(2,1)S(1)} %get-tuple-element.11.late_ref, bf16[512,512]{1,0:T(8,128)(2,1)S(1)} %copy-done.2, ...), custom_call_target="tpu_custom_call" | custom-call | flops 2147483648 | bytes 12582912 | tf_op jit(solution)/shard_map/middle/pallas_call | solution.py:231
  9.9 0.0 collective-permute-done.halo_ref
  10.0 2.3 %early.1 = (bf16[128,128,128]{2,1,0:T(8,128)(2,1)S(1)}, bf16[16,512,128]{2,1,0:T(8,128)(2,1)S(1)}) custom-call(s32[16,16,8,128]{3,2,1,0:T(8,128)S(1)} %get-tuple-element.12.head_ref, bf16[3,16,8,128]{3,2,1,0:T(8,128)(2,1)S(1)} %collective-permute-done.halo_ref, f32[64,128]{1,0:T(8,128)S(1)} %fusion.4.w_ref, ...), custom_call_target="tpu_custom_call", output_to_operand_aliasing={{1}: (6, {}), {0}: (7, {})} | custom-call | flops 2147483648 | bytes 8388608 | tf_op jit(solution)/shard_map/early/pallas_call | solution.py:247
  12.3 63.3 %all_to_all.5 = bf16[128,128,128]{2,1,0:T(8,128)(2,1)S(1)} all-to-all(bf16[128,128,128]{2,1,0:T(8,128)(2,1)S(1)} %get-tuple-element.16), channel_id=1, replica_groups=mesh['gx'=64,'ta'=2] {'gx','ta'}, dimensions={0} | all-to-all | bytes 8388608 | tf_op jit(solution)/shard_map/all_to_all | solution.py:287
  75.6 6.8 %gram.1 = f32[8,2,512,512]{3,2,1,0:T(8,128)} custom-call(bf16[64,2,128,128]{3,2,1,0:T(8,128)(2,1)S(1)} %bitcast.4), custom_call_target="tpu_custom_call" | custom-call | flops 4294967296 | bytes 20971520 | tf_op jit(solution)/shard_map/gram/pallas_call | solution.py:261
  (1 shorter events, 0.0 us)
Async XLA Ops:
  0.2 6.0 %copy-start = (bf16[1024,1024]{1,0:T(8,128)(2,1)S(1)}, bf16[1024,1024]{1,0:T(8,128)(2,1)}, u32[]{:S(2)}) copy-start(bf16[1024,1024]{1,0:T(8,128)(2,1)} %constant.66.clone.t2_ref) | copy-start | bytes 6291460
  0.3 6.0 %copy-start.1 = (bf16[512,512]{1,0:T(8,128)(2,1)S(1)}, bf16[512,512]{1,0:T(8,128)(2,1)}, u32[]{:S(2)}) copy-start(bf16[512,512]{1,0:T(8,128)(2,1)} %constant.65.clone.t1_ref) | copy-start | bytes 1572868
  0.3 6.0 %copy-start.2 = (bf16[512,512]{1,0:T(8,128)(2,1)S(1)}, bf16[512,512]{1,0:T(8,128)(2,1)}, u32[]{:S(2)}) copy-start(bf16[512,512]{1,0:T(8,128)(2,1)} %constant.64.clone.t0_ref) | copy-start | bytes 1572868
  3.7 6.3 %collective-permute-start = (bf16[3,16,8,128]{3,2,1,0:T(8,128)(2,1)S(1)}, bf16[3,16,8,128]{3,2,1,0:T(8,128)(2,1)S(1)}, u32[]{:S(2)}, u32[]{:S(2)}) collective-permute-start(bf16[3,16,8,128]{3,2,1,0:T(8,128)(2,1)S(1)} %get-tuple-element.13), channel_id=1, source_target_pairs={{0,1},{1,0},{2,3},{3,2},{4,5},{5,4},{6,7},{7,6},{8,9},{9,8},{10,11... | collective-permute-start | bytes 294920 | tf_op jit(solution)/shard_map/ppermute | solution.py:27

commit v6 on v5

--- a/solution.py
+++ b/solution.py
@@ -34,7 +34,8 @@
     positions = (tile * LANES + lane).astype(F32)
     centred = (positions + 0.5 - total_len / 2.0) / FRAME
     hamming = 0.54 - 0.46 * jnp.cos(2.0 * jnp.pi * positions / (total_len - 1))
-    return jnp.sinc(centred) * hamming
+    turn = jnp.pi * centred
+    return jnp.sin(turn) / turn * hamming
 
 
 def dft_rows(first, step, length):
@@ -111,7 +112,7 @@
                 emit(tasks[n - 1], part)
 
 
-def late_kernel(spec_here, v_hbm, w_ref, f_ref, tail_ref, frames, acc_even, acc_odd, sems):
+def late_kernel(spec_here, v_hbm, f_ref, tail_ref, w_ref, frames, acc_even, acc_odd, sems):
     begin = spec_here // 2 - (TAPS - 1)
     blocks = HALF // BLOCK
 
@@ -122,6 +123,7 @@
     fetch(0, TAPS - 1, blocks).start()
     for b in range(blocks):
         fetch(TAPS - 1 + b * BLOCK, BLOCK, b).start()
+    w_ref[...] = window_rows()
     fetch(0, TAPS - 1, blocks).wait()
 
     def step(b, carry):
@@ -183,16 +185,16 @@
         return real.reshape(INPUTS, LANES).astype(BF16), imag.reshape(INPUTS, LANES).astype(BF16)
 
     for group, channels in enumerate(((0, 4), (2, 6), (1, 3), (5, 7))):
-        for ta in range(2):
-            halves = [got_ref[:, ta, h * 64 + group * 16 : h * 64 + (group + 1) * 16, :].astype(F32) for h in range(2)]
-            for u in range(2):
-                mat = mats.at[u]
-                real, imag = sort(*[x[:, u * 8 : (u + 1) * 8, :] for x in halves])
+        for u, k in enumerate(channels):
+            mat = mats.at[u]
+            for ta in range(2):
+                rows = [slice(h * 64 + group * 16, h * 64 + (group + 1) * 16) for h in range(2)]
+                halves = [got_ref[:, ta, part, :].astype(F32)[:, u * 8 : (u + 1) * 8, :] for part in rows]
+                real, imag = sort(*halves)
                 mat[:INPUTS, ta * 128 : (ta + 1) * 128] = real
                 mat[:INPUTS, 256 + ta * 128 : 256 + (ta + 1) * 128] = imag
                 mat[INPUTS:, ta * 128 : (ta + 1) * 128] = imag
                 mat[INPUTS:, 256 + ta * 128 : 256 + (ta + 1) * 128] = -real
-        for u, k in enumerate(channels):
             for p in range(2):
                 left = mats[u, p * INPUTS : (p + 1) * INPUTS, :]
                 dims = (((1,), (1,)), ((), ()))
@@ -212,19 +214,23 @@
 RESULTS = [pltpu.VMEM((512 * 4, LANES), F32)] * 4
 
 
-def late_call(frames, window):
+def late_call(frames):
     return pl.pallas_call(
         functools.partial(late_kernel, frames.shape[0]),
-        out_shape=(FOLDED, jax.ShapeDtypeStruct((TAPS - 1, TILES, 8, LANES), BF16)),
-        in_specs=[ANY, VMEM],
-        out_specs=(VMEM, VMEM),
+        out_shape=(
+            FOLDED,
+            jax.ShapeDtypeStruct((TAPS - 1, TILES, 8, LANES), BF16),
+            jax.ShapeDtypeStruct((TAPS * TILES, LANES), F32),
+        ),
+        in_specs=[ANY],
+        out_specs=(VMEM, VMEM, VMEM),
         scratch_shapes=[pltpu.VMEM((HALF + TAPS - 1, TILES, 8, LANES), jnp.int32)]
         + ACCS
         + [pltpu.SemaphoreType.DMA((HALF // BLOCK + 1,))],
         compiler_params=pltpu.CompilerParams(vmem_limit_bytes=46 * MIB),
         cost_estimate=pl.CostEstimate(flops=8 * 1024 * 1024, bytes_accessed=4 * MIB, transcendentals=0),
         name="late",
-    )(frames, window)
+    )(frames)
 
 
 def middle_call(frames, window, late, tables):
@@ -278,9 +284,8 @@
     inputs_here, total_len = voltages.shape
     spec_here = total_len // FRAME
     frames = voltages.reshape(inputs_here, spec_here, TILES, LANES).transpose(1, 2, 0, 3)
-    window = window_rows()
     tables = [jnp.asarray(dft_rows(0, 4, 512)), jnp.asarray(dft_rows(2, 4, 512)), jnp.asarray(dft_rows(1, 2, 1024))]
-    late, tail = late_call(frames, window)
+    late, tail, window = late_call(frames)
     halo = halo_of(tail)
     payload, folded, head = middle_call(frames, window, late, tables)
     outgoing = early_call(head, halo, window, tables, folded, payload)

time: 82.5 us -> 82.2 us (level)
  no operation moved by 1% of the time
where the time goes in v6:
time: 82.2 us; the launch traced here: 82.1 us
  blocking collectives  63.3 us (77%)
  Pallas kernels  16.2 us (20%)
  starting transfers between devices  2.55 us (3%)
    all_to_all x1, blocking collectives, on_device(): lax.all_to_all(outgoing, ('gx', 'ta'), split_axis=0, concat_axis=0, tiled...  63.3 us
    pallas_call x1, Pallas kernels, gram_call(): pl.pallas_call(lambda *refs: gram_kernel(norm, *refs), out_shape=jax.Shap...  6.82 us
    pallas_call x1, Pallas kernels, middle_call(): pl.pallas_call(middle_kernel, out_shape=(PAYLOAD, FOLDED, jax.ShapeDtypeS...  3.72 us
    pallas_call x1, Pallas kernels, late_call(): pl.pallas_call(functools.partial(late_kernel, frames.shape[0]), out_shape...  3.38 us
    ppermute x1, starting transfers between devices, halo_of(): lax.ppermute(tail, 'ta', [(i, (i + 1) % count) for i in range(count)])  2.55 us
    pallas_call x1, Pallas kernels, early_call(): pl.pallas_call(early_kernel, out_shape=(PAYLOAD, FOLDED), in_specs=[VMEM]...  2.31 us
  transfers between devices with their start and end apart: 1, of which 0 were waited for; matrix products, arithmetic and copies ran while one was open for 0% of the time, Pallas kernels for 5%

profile of v6, /device:TPU:1, one launch (start us, length us, event | category | flops | bytes accessed | tf_op | source)
XLA Modules:
  0.0 82.1 jit_solution(3923674163233191438)
XLA Ops:
  0.0 0.0 copy-start
  0.0 0.0 copy-start.1
  0.0 0.0 copy-start.2
  0.0 3.4 %late.1 = (bf16[16,512,128]{2,1,0:T(8,128)(2,1)S(1)}, bf16[3,16,8,128]{3,2,1,0:T(8,128)(2,1)S(1)}, f32[64,128]{1,0:T(8,128)S(1)}) custom-call(s32[128,16,8,128]{3,2,1,0:T(8,128)} %bitcast.5), custom_call_target="tpu_custom_call" | custom-call | flops 8388608 | bytes 4194304 | tf_op jit(solution)/shard_map/late/pallas_call | solution.py:218
  3.4 2.5 %collective-permute-start = (bf16[3,16,8,128]{3,2,1,0:T(8,128)(2,1)S(1)}, bf16[3,16,8,128]{3,2,1,0:T(8,128)(2,1)S(1)}, u32[]{:S(2)}, u32[]{:S(2)}) collective-permute-start(bf16[3,16,8,128]{3,2,1,0:T(8,128)(2,1)S(1)} %get-tuple-element.15), channel_id=1, source_target_pairs={{0,1},{1,0},{2,3},{3,2},{4,5},{5,4},{6,7},{7,6},{8,9},{9,8},{10,11... | collective-permute-start | bytes 294920 | tf_op jit(solution)/shard_map/ppermute | solution.py:27
  5.9 0.0 copy-done
  5.9 0.0 copy-done.1
  5.9 0.0 copy-done.2
  6.0 3.7 %middle.1 = (bf16[128,128,128]{2,1,0:T(8,128)(2,1)S(1)}, bf16[16,512,128]{2,1,0:T(8,128)(2,1)S(1)}, s32[16,16,8,128]{3,2,1,0:T(8,128)S(1)}) custom-call(s32[128,16,8,128]{3,2,1,0:T(8,128)} %bitcast.6, f32[64,128]{1,0:T(8,128)S(1)} %get-tuple-element.12.w_ref, bf16[16,512,128]{2,1,0:T(8,128)(2,1)S(1)} %get-tuple-element.13.late_ref, ...), custom_call_target="tpu_custom_call" | custom-call | flops 2147483648 | bytes 12582912 | tf_op jit(solution)/shard_map/middle/pallas_call | solution.py:237
  9.7 0.0 collective-permute-done.halo_ref
  9.7 2.3 %early.1 = (bf16[128,128,128]{2,1,0:T(8,128)(2,1)S(1)}, bf16[16,512,128]{2,1,0:T(8,128)(2,1)S(1)}) custom-call(s32[16,16,8,128]{3,2,1,0:T(8,128)S(1)} %get-tuple-element.14.head_ref, bf16[3,16,8,128]{3,2,1,0:T(8,128)(2,1)S(1)} %collective-permute-done.halo_ref, f32[64,128]{1,0:T(8,128)S(1)} %get-tuple-element.12.w_ref, ...), custom_call_target="tpu_custom_call", output_to_operand_aliasing={{1}: (6, {}), {0}: (7, {})} | custom-call | flops 2147483648 | bytes 8388608 | tf_op jit(solution)/shard_map/early/pallas_call | solution.py:253
  12.0 63.3 %all_to_all.5 = bf16[128,128,128]{2,1,0:T(8,128)(2,1)S(1)} all-to-all(bf16[128,128,128]{2,1,0:T(8,128)(2,1)S(1)} %get-tuple-element.18), channel_id=1, replica_groups=mesh['gx'=64,'ta'=2] {'gx','ta'}, dimensions={0} | all-to-all | bytes 8388608 | tf_op jit(solution)/shard_map/all_to_all | solution.py:292
  75.3 6.8 %gram.1 = f32[8,2,512,512]{3,2,1,0:T(8,128)} custom-call(bf16[64,2,128,128]{3,2,1,0:T(8,128)(2,1)S(1)} %bitcast.4), custom_call_target="tpu_custom_call" | custom-call | flops 4294967296 | bytes 20971520 | tf_op jit(solution)/shard_map/gram/pallas_call | solution.py:267
Async XLA Ops:
  0.0 5.9 %copy-start = (bf16[1024,1024]{1,0:T(8,128)(2,1)S(1)}, bf16[1024,1024]{1,0:T(8,128)(2,1)}, u32[]{:S(2)}) copy-start(bf16[1024,1024]{1,0:T(8,128)(2,1)} %constant.8.clone.t2_ref) | copy-start | bytes 6291460
  0.0 5.9 %copy-start.1 = (bf16[512,512]{1,0:T(8,128)(2,1)S(1)}, bf16[512,512]{1,0:T(8,128)(2,1)}, u32[]{:S(2)}) copy-start(bf16[512,512]{1,0:T(8,128)(2,1)} %constant.7.clone.t1_ref) | copy-start | bytes 1572868
  0.0 5.9 %copy-start.2 = (bf16[512,512]{1,0:T(8,128)(2,1)S(1)}, bf16[512,512]{1,0:T(8,128)(2,1)}, u32[]{:S(2)}) copy-start(bf16[512,512]{1,0:T(8,128)(2,1)} %constant.6.clone.t0_ref) | copy-start | bytes 1572868
  3.4 6.3 %collective-permute-start = (bf16[3,16,8,128]{3,2,1,0:T(8,128)(2,1)S(1)}, bf16[3,16,8,128]{3,2,1,0:T(8,128)(2,1)S(1)}, u32[]{:S(2)}, u32[]{:S(2)}) collective-permute-start(bf16[3,16,8,128]{3,2,1,0:T(8,128)(2,1)S(1)} %get-tuple-element.15), channel_id=1, source_target_pairs={{0,1},{1,0},{2,3},{3,2},{4,5},{5,4},{6,7},{7,6},{8,9},{9,8},{10,11... | collective-permute-start | bytes 294920 | tf_op jit(solution)/shard_map/ppermute | solution.py:27

commit v7 on v6

--- a/solution.py
+++ b/solution.py
@@ -131,7 +131,7 @@
         filter_block(lambda f, tile: frames[b * BLOCK + f, tile], w_ref, (acc_even, acc_odd), f_ref, b)
         return carry
 
-    lax.fori_loop(0, blocks, step, 0)
+    lax.fori_loop(0, blocks, step, 0, unroll=True)
     keep = jnp.where(lax.axis_index("ta") == lax.axis_size("ta") - 1, 0.0, 1.0).astype(F32)
     for f in range(TAPS - 1):
         tail_ref[f] = (frames[HALF + f].astype(F32) * keep).astype(BF16)
@@ -158,7 +158,7 @@
         filter_block(lambda f, tile: frames[(b - 1) * BLOCK + f, tile], w_ref, (acc_even, acc_odd), f_ref, b)
         return carry
 
-    lax.fori_loop(1, blocks, step, 0)
+    lax.fori_loop(1, blocks, step, 0, unroll=True)
     head.wait()
 
 

time: 82.2 us -> 82.4 us (level)
  no operation moved by 1% of the time
where the time goes in v7:
time: 82.4 us; the launch traced here: 82.3 us
  blocking collectives  63.3 us (77%)
  Pallas kernels  16.3 us (20%)
  starting transfers between devices  2.55 us (3%)
    all_to_all x1, blocking collectives, on_device(): lax.all_to_all(outgoing, ('gx', 'ta'), split_axis=0, concat_axis=0, tiled...  63.3 us
    pallas_call x1, Pallas kernels, gram_call(): pl.pallas_call(lambda *refs: gram_kernel(norm, *refs), out_shape=jax.Shap...  6.82 us
    pallas_call x1, Pallas kernels, middle_call(): pl.pallas_call(middle_kernel, out_shape=(PAYLOAD, FOLDED, jax.ShapeDtypeS...  3.73 us
    pallas_call x1, Pallas kernels, late_call(): pl.pallas_call(functools.partial(late_kernel, frames.shape[0]), out_shape...  3.39 us
    ppermute x1, starting transfers between devices, halo_of(): lax.ppermute(tail, 'ta', [(i, (i + 1) % count) for i in range(count)])  2.55 us
    pallas_call x1, Pallas kernels, early_call(): pl.pallas_call(early_kernel, out_shape=(PAYLOAD, FOLDED), in_specs=[VMEM]...  2.32 us
  transfers between devices with their start and end apart: 1, of which 0 were waited for; matrix products, arithmetic and copies ran while one was open for 0% of the time, Pallas kernels for 5%

profile of v7, /device:TPU:1, one launch (start us, length us, event | category | flops | bytes accessed | tf_op | source)
XLA Modules:
  0.0 82.3 jit_solution(11580475935960210282)
XLA Ops:
  0.0 0.0 copy-start
  0.0 0.0 copy-start.1
  0.0 0.0 copy-start.2
  0.0 3.4 %late.1 = (bf16[16,512,128]{2,1,0:T(8,128)(2,1)S(1)}, bf16[3,16,8,128]{3,2,1,0:T(8,128)(2,1)S(1)}, f32[64,128]{1,0:T(8,128)S(1)}) custom-call(s32[128,16,8,128]{3,2,1,0:T(8,128)} %bitcast.5), custom_call_target="tpu_custom_call" | custom-call | flops 8388608 | bytes 4194304 | tf_op jit(solution)/shard_map/late/pallas_call | solution.py:218
  3.4 2.5 %collective-permute-start = (bf16[3,16,8,128]{3,2,1,0:T(8,128)(2,1)S(1)}, bf16[3,16,8,128]{3,2,1,0:T(8,128)(2,1)S(1)}, u32[]{:S(2)}, u32[]{:S(2)}) collective-permute-start(bf16[3,16,8,128]{3,2,1,0:T(8,128)(2,1)S(1)} %get-tuple-element.15), channel_id=1, source_target_pairs={{0,1},{1,0},{2,3},{3,2},{4,5},{5,4},{6,7},{7,6},{8,9},{9,8},{10,11... | collective-permute-start | bytes 294920 | tf_op jit(solution)/shard_map/ppermute | solution.py:27
  6.0 0.0 copy-done
  6.0 0.0 copy-done.1
  6.0 0.0 copy-done.2
  6.0 3.7 %middle.1 = (bf16[128,128,128]{2,1,0:T(8,128)(2,1)S(1)}, bf16[16,512,128]{2,1,0:T(8,128)(2,1)S(1)}, s32[16,16,8,128]{3,2,1,0:T(8,128)S(1)}) custom-call(s32[128,16,8,128]{3,2,1,0:T(8,128)} %bitcast.6, f32[64,128]{1,0:T(8,128)S(1)} %get-tuple-element.12.w_ref, bf16[16,512,128]{2,1,0:T(8,128)(2,1)S(1)} %get-tuple-element.13.late_ref, ...), custom_call_target="tpu_custom_call" | custom-call | flops 2147483648 | bytes 12582912 | tf_op jit(solution)/shard_map/middle/pallas_call | solution.py:237
  9.7 0.0 collective-permute-done.halo_ref
  9.7 2.3 %early.1 = (bf16[128,128,128]{2,1,0:T(8,128)(2,1)S(1)}, bf16[16,512,128]{2,1,0:T(8,128)(2,1)S(1)}) custom-call(s32[16,16,8,128]{3,2,1,0:T(8,128)S(1)} %get-tuple-element.14.head_ref, bf16[3,16,8,128]{3,2,1,0:T(8,128)(2,1)S(1)} %collective-permute-done.halo_ref, f32[64,128]{1,0:T(8,128)S(1)} %get-tuple-element.12.w_ref, ...), custom_call_target="tpu_custom_call", output_to_operand_aliasing={{1}: (6, {}), {0}: (7, {})} | custom-call | flops 2147483648 | bytes 8388608 | tf_op jit(solution)/shard_map/early/pallas_call | solution.py:253
  12.0 63.3 %all_to_all.5 = bf16[128,128,128]{2,1,0:T(8,128)(2,1)S(1)} all-to-all(bf16[128,128,128]{2,1,0:T(8,128)(2,1)S(1)} %get-tuple-element.18), channel_id=1, replica_groups=mesh['gx'=64,'ta'=2] {'gx','ta'}, dimensions={0} | all-to-all | bytes 8388608 | tf_op jit(solution)/shard_map/all_to_all | solution.py:292
  75.3 6.8 %gram.1 = f32[8,2,512,512]{3,2,1,0:T(8,128)} custom-call(bf16[64,2,128,128]{3,2,1,0:T(8,128)(2,1)S(1)} %bitcast.4), custom_call_target="tpu_custom_call" | custom-call | flops 4294967296 | bytes 20971520 | tf_op jit(solution)/shard_map/gram/pallas_call | solution.py:267
Async XLA Ops:
  0.0 6.0 %copy-start = (bf16[1024,1024]{1,0:T(8,128)(2,1)S(1)}, bf16[1024,1024]{1,0:T(8,128)(2,1)}, u32[]{:S(2)}) copy-start(bf16[1024,1024]{1,0:T(8,128)(2,1)} %constant.8.clone.t2_ref) | copy-start | bytes 6291460
  0.0 6.0 %copy-start.1 = (bf16[512,512]{1,0:T(8,128)(2,1)S(1)}, bf16[512,512]{1,0:T(8,128)(2,1)}, u32[]{:S(2)}) copy-start(bf16[512,512]{1,0:T(8,128)(2,1)} %constant.7.clone.t1_ref) | copy-start | bytes 1572868
  0.0 6.0 %copy-start.2 = (bf16[512,512]{1,0:T(8,128)(2,1)S(1)}, bf16[512,512]{1,0:T(8,128)(2,1)}, u32[]{:S(2)}) copy-start(bf16[512,512]{1,0:T(8,128)(2,1)} %constant.6.clone.t0_ref) | copy-start | bytes 1572868
  3.4 6.3 %collective-permute-start = (bf16[3,16,8,128]{3,2,1,0:T(8,128)(2,1)S(1)}, bf16[3,16,8,128]{3,2,1,0:T(8,128)(2,1)S(1)}, u32[]{:S(2)}, u32[]{:S(2)}) collective-permute-start(bf16[3,16,8,128]{3,2,1,0:T(8,128)(2,1)S(1)} %get-tuple-element.15), channel_id=1, source_target_pairs={{0,1},{1,0},{2,3},{3,2},{4,5},{5,4},{6,7},{7,6},{8,9},{9,8},{10,11... | collective-permute-start | bytes 294920 | tf_op jit(solution)/shard_map/ppermute | solution.py:27
